TPU v7x, 32 devices: a whole 2x2x4 slice. The times are simulated.
32 devices in a mesh: replica: 2 (over y), tensor: 16 (over z, x, core).
Axes of the slice: x: 2, y: 2, z: 4, core: 2. Of those that a mesh axis runs over, the one named last changes fastest.
Arguments:
- attn_out: bfloat16 [2, 768, 2048], P('replica', None, 'tensor'), may hold values from -6 to 6
- proj: bfloat16 [2, 2048, 2048], P('replica', 'tensor'), may hold values from -6 to 6
- momentum: bfloat16 [2, 2048, 2048], P('replica', 'tensor'), may hold values from -6 to 6
- target: bfloat16 [2, 768, 2048], P('replica'), may hold values from -6 to 6
- segment_ids: int32 [2, 768], P('replica'), may hold values from 0 to 95, never falling along the last dimension, each value on 1 to 192 neighbouring positions
- step: int32 [1], replicated, may hold values from 0 to 999
Outputs:
- projected: bfloat16 [2, 768, 2048], P('replica', 'tensor')
- attn_grad: bfloat16 [2, 768, 2048], P('replica', None, 'tensor')
- new_proj: bfloat16 [2, 2048, 2048], P('replica', 'tensor')
- new_moment: bfloat16 [2, 2048, 2048], P('replica', 'tensor')
All inputs are finite; a program needn't handle non-finite values.
Results may differ from a plain program's by a relative error of at most 0.0055.
Values may be sent and summed in bfloat16 or wider, within the bound.
A program may use at most 64 MiB of HBM per device.

v0:
```python
from functools import partial

import jax
import jax.numpy as jnp
from jax import lax
from jax.sharding import PartitionSpec as P

SEGS = 96


BETA_MOM = 0.9
STEP_RATE = 0.1


def as_sent(x):
    return jax.tree.map(lambda a: a.astype(jnp.bfloat16) if a.dtype == jnp.float32 else a, x)


def passed_along(x, axis, by):
    size = lax.axis_size(axis)
    return lax.ppermute(x, axis, [(i, (i + by) % size) for i in range(size)])


def send_partner(stacked, offset):
    return jax.tree.map(
        lambda part, own: part.astype(own.dtype),
        passed_along(as_sent(stacked), "replica", offset),
        stacked,
    )


def on_device(attn_out, proj, momentum, target, segment_ids, step):
    heads_in = attn_out[0]
    weight = proj[0]
    moment_in = momentum[0]
    target_rows = target[0]
    seg_rows = segment_ids[0]
    tokens_here = heads_in.shape[0]
    head_rows = weight.shape[0]
    tensor_size = lax.axis_size("tensor")
    rows_each = tokens_here // tensor_size
    scaling = (head_rows * tensor_size) ** (-0.5)
    same_doc = (seg_rows[:, None] == seg_rows[None, :]).astype(jnp.float32)
    doc_sizes = jnp.sum(same_doc, axis=1)
    weights = tokens_here / (SEGS * doc_sizes)
    first_row = lax.axis_index("tensor") * rows_each
    own_sums = lax.psum_scatter(
        jnp.dot(heads_in, weight, preferred_element_type=jnp.float32) * scaling,
        "tensor",
        scatter_dimension=0,
        tiled=True,
    )
    own_weights = lax.dynamic_slice_in_dim(weights, first_row, rows_each, 0)
    own_targets = lax.dynamic_slice_in_dim(target_rows, first_row, rows_each, 0)
    grad_shard = ((own_sums - own_targets.astype(jnp.float32)) * own_weights[:, None]).astype(
        jnp.bfloat16
    )
    grad_block = lax.all_gather(grad_shard, "tensor", axis=0, tiled=True)
    weight_sum = jnp.dot(heads_in.T, grad_block, preferred_element_type=jnp.float32)
    back_block = jnp.dot(grad_block, weight.T, preferred_element_type=jnp.float32)
    attn_grad = back_block
    projected = own_sums.astype(jnp.bfloat16)
    attn_grad = (attn_grad * scaling).astype(jnp.bfloat16)
    moment = (BETA_MOM * moment_in.astype(jnp.float32) + weight_sum * scaling).astype(jnp.bfloat16)
    updated = (weight.astype(jnp.float32) - STEP_RATE * moment.astype(jnp.float32)).astype(
        jnp.bfloat16
    )
    stacked = jnp.stack((updated, moment))
    levels = lax.axis_size("replica").bit_length() - 1
    chosen = step[0] % levels
    branches = [partial(send_partner, offset=1 << bit_pos) for bit_pos in range(levels)]
    partner = lax.switch(chosen, branches, stacked)
    mixed = ((stacked.astype(jnp.float32) + partner.astype(jnp.float32)) * 0.5).astype(jnp.bfloat16)
    return (projected[None], attn_grad[None], mixed[0][None], mixed[1][None])


def solution(mesh):
    return jax.shard_map(
        on_device,
        mesh=mesh,
        in_specs=(
            P("replica", None, "tensor"),
            P("replica", "tensor", None),
            P("replica", "tensor", None),
            P("replica", None, None),
            P("replica", None),
            P(),
        ),
        out_specs=(
            P("replica", "tensor", None),
            P("replica", None, "tensor"),
            P("replica", "tensor", None),
            P("replica", "tensor", None),
        ),
        check_vma=False,
    )
```

profile of v0, /device:TPU:0, one launch (start us, length us, event | category | flops | bytes accessed | tf_op | source)
XLA Modules:
  0.0 186.2 jit_solution(18059361390847897249)
XLA Ops:
  7.2 0.0 copy-start
  7.2 0.0 reduce-scatter.2.cloned.1.call-start
  7.2 0.9 copy-done
  8.1 4.7 %convolution_multiply_fusion = f32[768,2048]{1,0:T(8,128)} fusion(bf16[1,128,2048]{2,1,0:T(8,128)(2,1)} %param.7, bf16[1,768,128]{2,1,0:T(8,128)(2,1)S(1)} %copy-done), kind=kOutput, calls=%fused_computation | convolution fusion | flops 404226048 | bytes 7012352 | tf_op jit(solution)/shard_map/dot_general | solution.py:48
  12.8 0.0 copy-start.3
  12.8 0.0 copy-start.1
  12.8 0.0 copy-start.2
  12.8 0.0 reduce-scatter.2.cloned.1.call-update
  12.8 0.0 all-gather.2.cloned.1.call-start
  12.8 0.6 copy-done.3
  13.5 0.4 convert_reduce_fusion
  13.8 0.1 dynamic_slice.7
  13.9 86.9 %reduce-scatter.2.cloned.1.call-done = f32[48,2048]{1,0:T(8,128)} async-done(((f32[768,2048]{1,0:T(8,128)}), f32[48,2048]{1,0:T(8,128)}) %reduce-scatter.2.cloned.1.call-update) | async-done | bytes 393232 | tf_op jit(solution)/shard_map/reduce_scatter | solution.py:47
  100.9 1.9 %fusion.9 = (bf16[48,2048]{1,0:T(8,128)(2,1)}, bf16[1,48,2048]{2,1,0:T(8,128)(2,1)}) fusion(f32[48,2048]{1,0:T(8,128)} %reduce-scatter.2.cloned.1.call-done, f32[48]{0:T(128)S(1)} %dynamic_slice.7, bf16[1,768,2048]{2,1,0:T(8,128)(2,1)} %param.9, s32[]{:T(128)S(6)} %select_n.4), kind=kLoop, calls=%fused_computation.17 | loop fusion | flops 491520 | bytes 983236 | tf_op jit(solution)/shard_map/convert_element_type | solution.py:55
  102.8 0.0 all-gather.2.cloned.1.call-update
  102.8 0.0 copy-done.1
  102.8 0.3 copy.13
  103.1 0.0 copy-done.2
  103.1 0.3 copy.14
  103.4 44.9 %all-gather.2.cloned.1.call-done = bf16[768,2048]{1,0:T(8,128)(2,1)} async-done(((bf16[48,2048]{1,0:T(8,128)(2,1)}), bf16[768,2048]{1,0:T(8,128)(2,1)}) %all-gather.2.cloned.1.call-update) | async-done | bytes 3145744 | tf_op jit(solution)/shard_map/all_gather | solution.py:58
  148.3 2.9 %fusion.2 = bf16[128,2048]{0,1:T(8,128)(2,1)S(1)} fusion(bf16[768,2048]{1,0:T(8,128)(2,1)} %all-gather.2.cloned.1.call-done, bf16[1,128,2048]{1,2,0:T(8,128)(2,1)S(1)} %copy.14, bf16[1,768,128]{2,1,0:T(8,128)(2,1)S(1)} %copy-done), kind=kOutput, calls=%fused_computation.4 | convolution fusion | flops 403963904 | bytes 4390912 | tf_op jit(solution)/shard_map/dot_general | solution.py:59
  151.3 0.0 copy-start.4
  151.3 0.2 fusion.5
  151.4 0.1 pad_maximum_fusion
  151.6 1.5 collective-permute-start
  153.1 0.1 copy-done.4
  153.1 1.7 fusion.4
  154.8 22.1 %collective-permute-done = bf16[2,128,2048]{1,2,0:T(8,128)(2,1)S(1)} collective-permute-done((bf16[2,128,2048]{1,2,0:T(8,128)(2,1)S(1)}, bf16[2,128,2048]{1,2,0:T(8,128)(2,1)S(1)}, u32[]{:S(2)}, u32[]{:S(2)}) %collective-permute-start) | collective-permute-done | bytes 1048608 | tf_op jit(solution)/shard_map/ppermute | solution.py:21
  176.9 0.3 multiply_convert_fusion
  177.3 0.1 fusion.12
  177.4 1.0 copy.15
  178.4 1.0 copy.16
  (2 shorter events, 0.0 us)
Async XLA Ops:
  7.2 0.9 copy-start
  7.2 93.7 %reduce-scatter.2.cloned.1.call-start = ((), (), s32[]{:S(2)}) async-start(), calls=%async_computation.1 | async-start | bytes 6684672 | tf_op jit(solution)/shard_map/reduce_scatter | solution.py:47
  12.8 0.7 copy-start.3
  12.8 90.1 %copy-start.1 = (bf16[1,128,2048]{2,1,0:T(8,128)(2,1)S(1)}, bf16[1,128,2048]{2,1,0:T(8,128)(2,1)}, u32[]{:S(2)}) copy-start(bf16[1,128,2048]{2,1,0:T(8,128)(2,1)} %param.7) | copy-start | bytes 1572868
  12.8 90.4 %copy-start.2 = (bf16[1,128,2048]{2,1,0:T(8,128)(2,1)S(1)}, bf16[1,128,2048]{2,1,0:T(8,128)(2,1)}, u32[]{:S(2)}) copy-start(bf16[1,128,2048]{2,1,0:T(8,128)(2,1)} %param.8) | copy-start | bytes 1572868
  12.8 135.5 %all-gather.2.cloned.1.call-start = ((), (), s32[]{:S(2)}) async-start(), calls=%async_computation.2 | async-start | bytes 3342336 | tf_op jit(solution)/shard_map/all_gather | solution.py:58
  151.3 1.9 %copy-start.4 = (bf16[768,2048]{1,0:T(8,128)(2,1)S(1)}, bf16[768,2048]{1,0:T(8,128)(2,1)}, u32[]{:S(2)}) copy-start(bf16[768,2048]{1,0:T(8,128)(2,1)} %all-gather.2.cloned.1.call-done) | copy-start | bytes 9437188
  151.6 25.4 %collective-permute-start = (bf16[2,128,2048]{1,2,0:T(8,128)(2,1)S(1)}, bf16[2,128,2048]{1,2,0:T(8,128)(2,1)S(1)}, u32[]{:S(2)}, u32[]{:S(2)}) collective-permute-start(bf16[2,128,2048]{1,2,0:T(8,128)(2,1)S(1)} %pad_maximum_fusion), channel_id=1, source_target_pairs={{0,16},{16,0},{1,17},{17,1},{2,18},{18,2},{3,19},{19,3},{4,20},{20... | collective-permute-start | bytes 3145736 | tf_op jit(solution)/shard_map/ppermute | solution.py:21
Sparse Core Ops, SparseCore 0:
  12.9 87.9 reduce-scatter.1
  104.0 44.2 all-gather.1
where the time goes:
time: 187 us; the launch traced here: 186 us
  waiting for transfers between devices  154 us (82%)
  between operations  14.1 us (8%)
  matrix products  9.25 us (5%)
  local copies, waits for them, and re-layouts  4.25 us (2%)
  other arithmetic  2.94 us (2%)
    reduce_scatter x1, waiting for transfers between devices, on_device(): lax.psum_scatter(jnp.dot(heads_in, weight, preferred_element_type=jnp.flo...  86.9 us
    all_gather x1, waiting for transfers between devices, on_device(): grad_block = lax.all_gather(grad_shard, 'tensor', axis=0, tiled=True)  44.9 us
    ppermute x1, waiting for transfers between devices, passed_along(): return lax.ppermute(x, axis, [(i, (i + by) % size) for i in range(size)])  22.1 us
    dot_general x1, matrix products, on_device(): jnp.dot(heads_in, weight, preferred_element_type=jnp.float32) * scaling  4.66 us
    unnamed x14, local copies, waits for them, and re-layouts  4.1 us
  transfers between devices with their start and end apart: 3, of which 3 were waited for; matrix products, arithmetic and copies ran while one was open for 1% of the time, Pallas kernels for 0%

commit v1 on v0

v1 whole, which is shorter than its diff:
```python
import functools
from functools import partial

import jax
import jax.numpy as jnp
from jax import lax
from jax.experimental import pallas as pl
from jax.experimental.pallas import tpu as pltpu
from jax.sharding import PartitionSpec as P

SEGS = 96
BETA_MOM = 0.9
STEP_RATE = 0.1
CHUNKS = 8
BF16 = jnp.bfloat16
F32 = jnp.float32
MESH = pl.DeviceIdType.MESH


def radices_of(size):
    found = []
    while size > 4 and size % 2 == 0:
        found.append(2)
        size //= 2
    if size > 1:
        found.append(size)
    return tuple(found)


def kernel(
    radices,
    replicas,
    chunks,
    mixing,
    scaling,
    attn_ref,
    proj_ref,
    mom_ref,
    seg_ref,
    target_ref,
    projected_ref,
    attn_grad_ref,
    out_proj_ref,
    out_mom_ref,
    *scratch,
):
    levels = len(radices)
    sums = scratch[:levels]
    landed = scratch[levels : 2 * levels]
    (
        grads,
        moments,
        partner_moments,
        partner_proj,
        own_target,
        attn_t,
        total,
        rs_send,
        rs_recv,
        ag_send,
        ag_recv,
        y_send,
        y_recv,
        local_sem,
    ) = scratch[2 * levels :]
    tokens, depth = attn_ref.shape
    width = proj_ref.shape[1] // chunks
    rows = own_target.shape[0]
    me = lax.axis_index("tensor")
    rep = lax.axis_index("replica")
    digits, strides, rest, stride = [], [], me, 1
    for radix in radices:
        digits.append(lax.rem(rest, radix))
        strides.append(stride)
        rest = lax.div(rest, radix)
        stride *= radix

    def peer(level, by):
        to = lax.rem(digits[level] + by, radices[level])
        return to, {"tensor": me + (to - digits[level]) * strides[level]}

    other = {"replica": lax.rem(rep + 1, replicas)}

    barrier = pltpu.get_barrier_semaphore()
    greeted = 0
    for level in range(levels):
        for by in range(1, radices[level]):
            pl.semaphore_signal(barrier, inc=1, device_id=peer(level, by)[1], device_id_type=MESH)
            greeted += 1
    if mixing:
        pl.semaphore_signal(barrier, inc=1, device_id=other, device_id_type=MESH)
        greeted += 1
    fetch = pltpu.make_async_copy(target_ref.at[me], own_target, local_sem)
    fetch.start()

    def columns(k):
        return slice(k * width, (k + 1) * width)

    def product(k):
        part = jnp.dot(attn_ref[...], proj_ref[:, columns(k)], preferred_element_type=F32)
        shape = tuple(reversed(radices)) + (rows, width)
        sums[0][k] = part.reshape(shape).astype(BF16)

    product(0)
    attn_t[...] = attn_ref[...].T
    total[...] = jnp.zeros_like(total)
    pl.semaphore_wait(barrier, greeted)

    proj_copy = None
    if mixing:
        proj_copy = pltpu.make_async_remote_copy(
            src_ref=proj_ref,
            dst_ref=partner_proj,
            send_sem=y_send.at[chunks],
            recv_sem=y_recv.at[chunks],
            device_id=other,
            device_id_type=MESH,
        )
        proj_copy.start()

    seg = seg_ref[...].astype(F32)
    shape = (rows, tokens)
    row_at = lax.broadcasted_iota(jnp.int32, shape, 0) + me * rows
    col_at = lax.broadcasted_iota(jnp.int32, shape, 1)
    seg_all = jnp.broadcast_to(seg, shape)
    own_seg = jnp.sum(jnp.where(row_at == col_at, seg_all, 0.0), axis=1, keepdims=True)
    count = jnp.sum(jnp.where(seg_all == own_seg, 1.0, 0.0), axis=1, keepdims=True)
    weights = tokens / (SEGS * count)

    copies = {}

    def rs_start(level, k):
        high = (slice(None),) * (levels - 1 - level)
        for by in range(1, radices[level]):
            to, device = peer(level, by)
            copy = pltpu.make_async_remote_copy(
                src_ref=sums[level].at[(k,) + high + (to,)],
                dst_ref=landed[level].at[k, by - 1],
                send_sem=rs_send.at[level, k, by - 1],
                recv_sem=rs_recv.at[level, k, by - 1],
                device_id=device,
                device_id_type=MESH,
            )
            copy.start()
            copies["rs", level, k, by] = copy

    def ag_start(level, k):
        high = (slice(None),) * (levels - 1 - level)
        place = (k,) + high + tuple(digits[i] for i in range(level, -1, -1))
        for by in range(1, radices[level]):
            copy = pltpu.make_async_remote_copy(
                src_ref=grads.at[place],
                dst_ref=grads.at[place],
                send_sem=ag_send.at[level, k, by - 1],
                recv_sem=ag_recv.at[level, k, by - 1],
                device_id=peer(level, by)[1],
                device_id_type=MESH,
            )
            copy.start()
            copies["ag", level, k, by] = copy

    def wait_recv(kind, level, k):
        for by in range(1, radices[level]):
            copies[kind, level, k, by].wait_recv()

    def first(k):
        if k > 0:
            product(k)
        rs_start(0, k)

    def reduce_stage(level, k):
        wait_recv("rs", level, k)
        high = (slice(None),) * (levels - 1 - level)
        value = sums[level][(k,) + high + (digits[level],)].astype(F32)
        for by in range(1, radices[level]):
            value = value + landed[level][k, by - 1].astype(F32)
        if level + 1 < levels:
            sums[level + 1][k] = value.astype(BF16)
            rs_start(level + 1, k)
            return
        if k == 0:
            fetch.wait()
        summed = value * scaling
        projected_ref[:, columns(k)] = summed.astype(BF16)
        grad = (summed - own_target[:, columns(k)].astype(F32)) * weights
        grads[(k,) + tuple(reversed(digits))] = grad.astype(BF16)
        ag_start(levels - 1, k)

    def gather_stage(level, k):
        wait_recv("ag", level, k)
        if level > 0:
            ag_start(level - 1, k)
            return
        block = grads[k]
        if rows % 16:
            block = block.astype(F32).reshape(tokens, width).astype(BF16)
        else:
            block = block.reshape(tokens, width)
        gradient = jnp.dot(attn_t[...], block, preferred_element_type=F32) * scaling
        moment = (BETA_MOM * mom_ref[:, columns(k)].astype(F32) + gradient).astype(BF16)
        if mixing:
            moments[k] = moment
            copy = pltpu.make_async_remote_copy(
                src_ref=moments.at[k],
                dst_ref=partner_moments.at[k],
                send_sem=y_send.at[k],
                recv_sem=y_recv.at[k],
                device_id=other,
                device_id_type=MESH,
            )
            copy.start()
            copies["y", k] = copy
        else:
            out_mom_ref[:, columns(k)] = moment
            out_proj_ref[:, columns(k)] = updated_of(proj_ref[:, columns(k)], moment)
        total[...] += lax.dot_general(
            block, proj_ref[:, columns(k)], (((1,), (1,)), ((), ())), preferred_element_type=F32
        )

    def updated_of(weight, moment):
        return (weight.astype(F32) - STEP_RATE * moment.astype(F32)).astype(BF16)

    def mix_stage(k):
        if not mixing:
            return
        if k == 0:
            proj_copy.wait_recv()
        copies["y", k].wait_recv()
        own, theirs = moments[k], partner_moments[k]
        out_mom_ref[:, columns(k)] = ((own.astype(F32) + theirs.astype(F32)) * 0.5).astype(BF16)
        one = updated_of(proj_ref[:, columns(k)], own).astype(F32)
        two = updated_of(partner_proj[:, columns(k)], theirs).astype(F32)
        out_proj_ref[:, columns(k)] = ((one + two) * 0.5).astype(BF16)

    stages = [first]
    stages += [partial(reduce_stage, level) for level in range(levels)]
    stages += [partial(gather_stage, level) for level in range(levels - 1, -1, -1)]
    stages += [mix_stage]
    for step in range(chunks + len(stages) - 1):
        for j, stage in enumerate(stages):
            if 0 <= step - j < chunks:
                stage(step - j)

    attn_grad_ref[...] = (total[...] * scaling).astype(BF16)
    for copy in copies.values():
        copy.wait_send()
    if mixing:
        proj_copy.wait_send()


def fused(attn, proj, mom, seg, target, radices, replicas, mixing):
    tokens, depth = attn.shape
    wide = proj.shape[1]
    size = 1
    for radix in radices:
        size *= radix
    rows = tokens // size
    chunks = CHUNKS
    width = wide // chunks
    levels = len(radices)
    most = max(radices) - 1
    scaling = (depth * size) ** (-0.5)
    sums, landed = [], []
    for level in range(levels):
        high = tuple(reversed(radices[level + 1 :]))
        sums.append(pltpu.VMEM((chunks,) + high + (radices[level], rows, width), BF16))
        landed.append(pltpu.VMEM((chunks, radices[level] - 1) + high + (rows, width), BF16))
    vmem = pl.BlockSpec(memory_space=pltpu.VMEM)
    return pl.pallas_call(
        functools.partial(kernel, radices, replicas, chunks, mixing, scaling),
        out_shape=(
            jax.ShapeDtypeStruct((rows, wide), BF16),
            jax.ShapeDtypeStruct((tokens, depth), BF16),
            jax.ShapeDtypeStruct((depth, wide), BF16),
            jax.ShapeDtypeStruct((depth, wide), BF16),
        ),
        in_specs=[vmem, vmem, vmem, vmem, pl.BlockSpec(memory_space=pl.ANY)],
        out_specs=(vmem, vmem, vmem, vmem),
        scratch_shapes=sums
        + landed
        + [
            pltpu.VMEM((chunks,) + tuple(reversed(radices)) + (rows, width), BF16),
            pltpu.VMEM((chunks, depth, width), BF16),
            pltpu.VMEM((chunks, depth, width), BF16),
            pltpu.VMEM((depth, wide), BF16),
            pltpu.VMEM((rows, wide), BF16),
            pltpu.VMEM((depth, tokens), BF16),
            pltpu.VMEM((tokens, depth), F32),
            pltpu.SemaphoreType.DMA((levels, chunks, most)),
            pltpu.SemaphoreType.DMA((levels, chunks, most)),
            pltpu.SemaphoreType.DMA((levels, chunks, most)),
            pltpu.SemaphoreType.DMA((levels, chunks, most)),
            pltpu.SemaphoreType.DMA((chunks + 1,)),
            pltpu.SemaphoreType.DMA((chunks + 1,)),
            pltpu.SemaphoreType.DMA,
        ],
        cost_estimate=pl.CostEstimate(
            flops=6 * tokens * depth * wide, bytes_accessed=8 * depth * wide, transcendentals=0
        ),
        compiler_params=pltpu.CompilerParams(
            collective_id=0, has_side_effects=True, vmem_limit_bytes=48 * 1024 * 1024
        ),
    )(attn, proj, mom, seg, target)


def passed_along(x, axis, by):
    size = lax.axis_size(axis)
    return lax.ppermute(x, axis, [(i, (i + by) % size) for i in range(size)])


def on_device(attn_out, proj, momentum, target, segment_ids, step):
    tensor_size = lax.axis_size("tensor")
    replicas = lax.axis_size("replica")
    rows_each = target.shape[1] // tensor_size
    bits = replicas.bit_length() - 1
    projected, attn_grad, updated, moment = fused(
        attn_out[0],
        proj[0],
        momentum[0],
        segment_ids,
        target[0].reshape(tensor_size, rows_each, target.shape[2]),
        radices_of(tensor_size),
        replicas,
        replicas == 2,
    )
    if replicas > 2:
        stacked = jnp.stack((updated, moment))
        branches = [
            partial(passed_along, axis="replica", by=1 << bit_pos) for bit_pos in range(bits)
        ]
        partner = lax.switch(step[0] % bits, branches, stacked)
        mixed = ((stacked.astype(F32) + partner.astype(F32)) * 0.5).astype(BF16)
        updated, moment = mixed[0], mixed[1]
    return (projected[None], attn_grad[None], updated[None], moment[None])


def solution(mesh):
    return jax.shard_map(
        on_device,
        mesh=mesh,
        in_specs=(
            P("replica", None, "tensor"),
            P("replica", "tensor", None),
            P("replica", "tensor", None),
            P("replica", None, None),
            P("replica", None),
            P(),
        ),
        out_specs=(
            P("replica", "tensor", None),
            P("replica", None, "tensor"),
            P("replica", "tensor", None),
            P("replica", "tensor", None),
        ),
        check_vma=False,
    )
```

time: 187 us -> 70.5 us (0.38)
  waiting for transfers between devices: 154 us -> 0 us
  Pallas kernels: 0 us -> 61 us
  between operations: 14.1 us -> 0.65 us
  matrix products: 9.25 us -> 0 us
  local copies, waits for them, and re-layouts: 4.25 us -> 8.52 us
  other arithmetic: 2.94 us -> 0 us
    reduce_scatter x1 -> x0, waiting for transfers between devices: 86.9 us -> none  [on_device(): lax.psum_scatter(jnp.dot(heads_in, weight, preferred_element_type=jnp.flo...]
    pallas_call x0 -> x1, Pallas kernels: none -> 61 us  [fused(): pl.pallas_call(functools.partial(kernel, radices, replicas, chunks, mixin...]
    all_gather x1 -> x0, waiting for transfers between devices: 44.9 us -> none  [on_device(): grad_block = lax.all_gather(grad_shard, 'tensor', axis=0, tiled=True)]
    ppermute x1 -> x0, waiting for transfers between devices: 22.1 us -> none  [passed_along(): return lax.ppermute(x, axis, [(i, (i + by) % size) for i in range(size)])]
    dot_general x3 -> x0, matrix products: 9.25 us -> none  [the longest x1 4.66 us: on_device(): jnp.dot(heads_in, weight, preferred_element_type=jnp.float32) * scaling]
    unnamed x14, local copies, waits for them, and re-layouts: 4.1 us -> 8.52 us
    convert_element_type x2 -> x0, other arithmetic: 2.27 us -> none  [the longest x1 1.93 us: on_device(): ((own_sums - own_targets.astype(jnp.float32)) * own_weights[:, None]).ast...]
  transfers between devices with their start and end apart: 3 -> 0, of which waited for: 3 -> 0; matrix products, arithmetic and copies ran while one was open for 1% -> 0% of each run, Pallas kernels for 0% -> 0%
where the time goes in v1:
time: 70.5 us; the launch traced here: 70.2 us
  Pallas kernels  61 us (87%)
  local copies, waits for them, and re-layouts  8.52 us (12%)
    pallas_call x1, Pallas kernels, fused(): pl.pallas_call(functools.partial(kernel, radices, replicas, chunks, mixin...  61 us
    unnamed x14, local copies, waits for them, and re-layouts  8.52 us

profile of v1, /device:TPU:0, one launch (start us, length us, event | category | flops | bytes accessed | tf_op | source)
XLA Modules:
  0.0 70.2 jit_solution(16803922086117571261)
XLA Ops:
  0.6 0.0 copy-start
  0.6 1.9 %copy-done = bf16[1,768,2048]{2,1,0:T(8,128)(2,1)S(1)} copy-done((bf16[1,768,2048]{2,1,0:T(8,128)(2,1)S(1)}, bf16[1,768,2048]{2,1,0:T(8,128)(2,1)}, u32[]{:S(2)}) %copy-start) | copy-done | bytes 3145752
  2.5 0.0 copy-start.1
  2.5 1.0 %copy-done.1 = bf16[1,128,2048]{2,1,0:T(8,128)(2,1)S(1)} copy-done((bf16[1,128,2048]{2,1,0:T(8,128)(2,1)S(1)}, bf16[1,128,2048]{2,1,0:T(8,128)(2,1)}, u32[]{:S(2)}) %copy-start.1) | copy-done | bytes 524312
  3.6 0.0 copy-start.2
  3.6 1.0 %copy-done.2 = bf16[1,128,2048]{2,1,0:T(8,128)(2,1)S(1)} copy-done((bf16[1,128,2048]{2,1,0:T(8,128)(2,1)S(1)}, bf16[1,128,2048]{2,1,0:T(8,128)(2,1)}, u32[]{:S(2)}) %copy-start.2) | copy-done | bytes 524312
  4.6 0.0 copy-start.3
  4.6 0.9 %copy-done.3 = bf16[1,768,128]{2,1,0:T(8,128)(2,1)S(1)} copy-done((bf16[1,768,128]{2,1,0:T(8,128)(2,1)S(1)}, bf16[1,768,128]{2,1,0:T(8,128)(2,1)}, u32[]{:S(2)}) %copy-start.3) | copy-done | bytes 196632
  5.5 0.0 copy-start.4
  5.5 0.7 copy-done.4
  6.2 61.0 %shard_map.84 = (bf16[48,2048]{1,0:T(8,128)(2,1)S(1)}, bf16[768,128]{1,0:T(8,128)(2,1)S(1)}, bf16[128,2048]{1,0:T(8,128)(2,1)S(1)}, bf16[128,2048]{1,0:T(8,128)(2,1)S(1)}) custom-call(bf16[768,128]{1,0:T(8,128)(2,1)S(1)} %bitcast.15, bf16[128,2048]{1,0:T(8,128)(2,1)S(1)} %bitcast.13, bf16[128,2048]{1,0:T(8,128)(2,1)S(1)} %bitcast.14, ...), custom_call_target="tpu_custom_call" | custom-call | flops 1207959552 | bytes 2097152 | tf_op jit(solution)/shard_map/pallas_call | solution.py:269
  67.3 0.7 copy.13
  67.9 0.7 copy.14
  68.6 0.8 %copy.15 = bf16[1,128,2048]{2,1,0:T(8,128)(2,1)} copy(bf16[1,128,2048]{2,1,0:T(8,128)(2,1)S(1)} %bitcast.9) | data formatting | bytes 1048576
  69.4 0.8 %copy.16 = bf16[1,128,2048]{2,1,0:T(8,128)(2,1)} copy(bf16[1,128,2048]{2,1,0:T(8,128)(2,1)S(1)} %bitcast.8) | data formatting | bytes 1048576
Async XLA Ops:
  0.6 1.9 %copy-start = (bf16[1,768,2048]{2,1,0:T(8,128)(2,1)S(1)}, bf16[1,768,2048]{2,1,0:T(8,128)(2,1)}, u32[]{:S(2)}) copy-start(bf16[1,768,2048]{2,1,0:T(8,128)(2,1)} %param.9) | copy-start | bytes 9437188
  2.5 1.0 %copy-start.1 = (bf16[1,128,2048]{2,1,0:T(8,128)(2,1)S(1)}, bf16[1,128,2048]{2,1,0:T(8,128)(2,1)}, u32[]{:S(2)}) copy-start(bf16[1,128,2048]{2,1,0:T(8,128)(2,1)} %param.7) | copy-start | bytes 1572868
  3.6 1.0 %copy-start.2 = (bf16[1,128,2048]{2,1,0:T(8,128)(2,1)S(1)}, bf16[1,128,2048]{2,1,0:T(8,128)(2,1)}, u32[]{:S(2)}) copy-start(bf16[1,128,2048]{2,1,0:T(8,128)(2,1)} %param.8) | copy-start | bytes 1572868
  4.6 0.9 %copy-start.3 = (bf16[1,768,128]{2,1,0:T(8,128)(2,1)S(1)}, bf16[1,768,128]{2,1,0:T(8,128)(2,1)}, u32[]{:S(2)}) copy-start(bf16[1,768,128]{2,1,0:T(8,128)(2,1)} %param.6) | copy-start | bytes 589828
  5.5 0.7 copy-start.4

commit v2 on v0

v2 whole, which is shorter than its diff:
```python
import functools
import itertools
from functools import partial

import jax
import jax.numpy as jnp
from jax import lax
from jax.experimental import pallas as pl
from jax.experimental.pallas import tpu as pltpu
from jax.sharding import PartitionSpec as P

SEGS = 96
BETA_MOM = 0.9
STEP_RATE = 0.1
CHUNKS = 8
AHEAD = 4
VMEM_BYTES = 63 * 1024 * 1024
BF16 = jnp.bfloat16
F32 = jnp.float32
MESH = pl.DeviceIdType.MESH


def radices_of(size):
    found = []
    while size > 2 and size % 2 == 0:
        found.append(2)
        size //= 2
    if size > 1:
        found.append(size)
    return tuple(found)


def kernel(
    radices,
    local,
    replicas,
    chunks,
    mixing,
    scaling,
    attn_hbm,
    proj_hbm,
    mom_hbm,
    seg_ref,
    target_hbm,
    projected_hbm,
    attn_grad_hbm,
    out_proj_hbm,
    out_mom_hbm,
    *scratch,
):
    levels = len(radices)
    outer = levels - local
    sums = scratch[:outer]
    landed = scratch[outer : 2 * outer]
    (
        attn,
        attn_group,
        proj,
        mom,
        target,
        grads,
        moments,
        partner_moments,
        partner_proj,
        attn_t,
        total,
        projected,
        attn_grad,
        out_proj,
        out_mom,
        in_sem,
        proj_sem,
        out_sem,
        a_send,
        a_recv,
        p_send,
        p_recv,
        rs_send,
        rs_recv,
        ag_send,
        ag_recv,
        y_send,
        y_recv,
    ) = scratch[2 * outer :]
    rows, depth = attn.shape[-2:]
    width = proj.shape[-1]
    me = lax.axis_index("tensor")
    rep = lax.axis_index("replica")
    digits, strides, rest, stride = [], [], me, 1
    for radix in radices:
        digits.append(lax.rem(rest, radix))
        strides.append(stride)
        rest = lax.div(rest, radix)
        stride *= radix
    tokens = stride * rows
    mine = tuple(reversed(digits))
    own = tuple(reversed(digits[:local]))
    outer_all = (slice(None),) * outer

    def peer(level, by):
        to = lax.rem(digits[level] + by, radices[level])
        return to, me + (to - digits[level]) * strides[level]

    group = []
    for offsets in itertools.product(*[range(r) for r in reversed(radices[:local])]):
        if any(offsets):
            there, index = [], me
            for level, by in zip(range(local - 1, -1, -1), offsets):
                to, _ = peer(level, by)
                there.append(to)
                index = index + (to - digits[level]) * strides[level]
            group.append((tuple(there), index))

    other = {"replica": lax.rem(rep + 1, replicas)}

    def columns(k):
        return slice(k * width, (k + 1) * width)

    loads = [
        pltpu.make_async_copy(attn_hbm, attn, in_sem.at[0]),
        pltpu.make_async_copy(mom_hbm, mom, in_sem.at[1]),
        pltpu.make_async_copy(target_hbm.at[me], target, in_sem.at[2]),
    ]
    proj_loads = [
        pltpu.make_async_copy(proj_hbm.at[:, columns(k)], proj.at[(k,) + own], proj_sem.at[k])
        for k in range(chunks)
    ]
    loads[0].start()
    for load in proj_loads:
        load.start()
    loads[1].start()
    loads[2].start()

    barrier = pltpu.get_barrier_semaphore()
    greet = [{"tensor": index} for _, index in group]
    for level in range(local, levels):
        greet += [{"tensor": peer(level, by)[1]} for by in range(1, radices[level])]
    if mixing:
        greet.append(other)
    for device in greet:
        pl.semaphore_signal(barrier, inc=1, device_id=device, device_id_type=MESH)
    loads[0].wait()
    pl.semaphore_wait(barrier, len(greet))

    copies = {}

    def send(key, src, dst, send_sem, recv_sem, device):
        copy = pltpu.make_async_remote_copy(
            src_ref=src,
            dst_ref=dst,
            send_sem=send_sem,
            recv_sem=recv_sem,
            device_id=device,
            device_id_type=MESH,
        )
        copy.start()
        copies[key] = copy

    for i, (there, index) in enumerate(group):
        send(
            ("a", i),
            attn.at[outer_all + there],
            attn_group.at[own],
            a_send.at[i],
            a_recv.at[i],
            {"tensor": index},
        )

    def gather(kind, ref, sems, level, k, high):
        place = (k,) + high + tuple(digits[i] for i in range(level, -1, -1))
        for by in range(1, radices[level]):
            send(
                (kind, level, k, by),
                ref.at[place],
                ref.at[place],
                sems[0].at[level, k, by - 1],
                sems[1].at[level, k, by - 1],
                {"tensor": peer(level, by)[1]},
            )

    def share_proj(level, k):
        gather("p", proj, (p_send, p_recv), level, k, (slice(None),) * (local - 1 - level))

    def share_grad(level, k):
        gather("g", grads, (ag_send, ag_recv), level, k, (slice(None),) * (levels - 1 - level))

    def reduce_start(level, k):
        high = (slice(None),) * (levels - 1 - level)
        for by in range(1, radices[level]):
            to, index = peer(level, by)
            send(
                ("r", level, k, by),
                sums[level - local].at[(k,) + high + (to,)],
                landed[level - local].at[k, by - 1],
                rs_send.at[level, k, by - 1],
                rs_recv.at[level, k, by - 1],
                {"tensor": index},
            )

    def wait_recv(kind, level, k):
        for by in range(1, radices[level]):
            copies[kind, level, k, by].wait_recv()

    def first(k):
        proj_loads[k].wait()
        if local > 0:
            share_proj(local - 1, k)

    def proj_stage(level, k):
        wait_recv("p", level, k)
        share_proj(level - 1, k)

    def product(k):
        if local > 0:
            wait_recv("p", 0, k)
        if k == 0:
            for i in range(len(group)):
                copies["a", i].wait_recv()
        part = jnp.zeros((tokens // len_group, width), F32)
        for at in itertools.product(*[range(r) for r in reversed(radices[:local])]):
            left = attn_group[at]
            part = part + jnp.dot(flat(left), proj[(k,) + at], preferred_element_type=F32)
        shape = tuple(reversed(radices[local:])) + (rows, width)
        part = part.reshape(shape)
        if outer > 0:
            sums[0][k] = part.astype(BF16)
            reduce_start(local, k)
        else:
            finish(part, k)

    def flat(block):
        count = 1
        for n in block.shape[:-1]:
            count *= n
        if rows % 16:
            return block.astype(F32).reshape(count, block.shape[-1]).astype(BF16)
        return block.reshape(count, block.shape[-1])

    def reduce_stage(level, k):
        wait_recv("r", level, k)
        high = (slice(None),) * (levels - 1 - level)
        value = sums[level - local][(k,) + high + (digits[level],)].astype(F32)
        for by in range(1, radices[level]):
            value = value + landed[level - local][k, by - 1].astype(F32)
        if level + 1 < levels:
            sums[level + 1 - local][k] = value.astype(BF16)
            reduce_start(level + 1, k)
        else:
            finish(value, k)

    def finish(value, k):
        if k == 0:
            loads[2].wait()
        summed = value * scaling
        grad = (summed - target[:, columns(k)].astype(F32)) * weights
        grads[(k,) + mine] = grad.astype(BF16)
        share_grad(levels - 1, k)
        projected[k] = summed.astype(BF16)
        store(("projected", k), projected.at[k], projected_hbm.at[:, columns(k)], 3 * k)

    stores = []

    def store(key, src, dst, place):
        copy = pltpu.make_async_copy(src, dst, out_sem.at[place])
        copy.start()
        stores.append(copy)

    def gather_stage(level, k):
        wait_recv("g", level, k)
        if level > 0:
            share_grad(level - 1, k)
            return
        if k == 0:
            loads[1].wait()
        block = flat(grads[k])
        weight = proj[(k,) + own]
        gradient = jnp.dot(attn_t[...], block, preferred_element_type=F32) * scaling
        moment = (BETA_MOM * mom[:, columns(k)].astype(F32) + gradient).astype(BF16)
        if mixing:
            moments[k] = moment
            send(
                ("y", k),
                moments.at[k],
                partner_moments.at[k],
                y_send.at[k],
                y_recv.at[k],
                other,
            )
        else:
            put(k, updated_of(weight, moment), moment)
        total[...] += lax.dot_general(
            block, weight, (((1,), (1,)), ((), ())), preferred_element_type=F32
        )

    def put(k, new_proj, new_moment):
        out_proj[k] = new_proj
        out_mom[k] = new_moment
        store(("proj", k), out_proj.at[k], out_proj_hbm.at[:, columns(k)], 3 * k + 1)
        store(("mom", k), out_mom.at[k], out_mom_hbm.at[:, columns(k)], 3 * k + 2)

    def updated_of(weight, moment):
        return (weight.astype(F32) - STEP_RATE * moment.astype(F32)).astype(BF16)

    def mix_stage(k):
        if not mixing:
            return
        if k == 0:
            copies["yp"].wait_recv()
        copies["y", k].wait_recv()
        ours, theirs = moments[k], partner_moments[k]
        one = updated_of(proj[(k,) + own], ours).astype(F32)
        two = updated_of(partner_proj[:, columns(k)], theirs).astype(F32)
        put(
            k,
            ((one + two) * 0.5).astype(BF16),
            ((ours.astype(F32) + theirs.astype(F32)) * 0.5).astype(BF16),
        )

    len_group = len(group) + 1
    stages = [first]
    stages += [partial(proj_stage, level) for level in range(local - 1, 0, -1)]
    stages += [product]
    stages += [partial(reduce_stage, level) for level in range(local, levels)]
    stages += [partial(gather_stage, level) for level in range(levels - 1, -1, -1)]
    stages += [mix_stage]

    ahead = min(AHEAD, chunks)
    for k in range(ahead):
        first(k)
    if mixing:
        send(
            "yp",
            proj_hbm,
            partner_proj,
            y_send.at[chunks],
            y_recv.at[chunks],
            other,
        )
    attn_group[own] = attn[outer_all + own]

    seg = seg_ref[...].astype(F32)
    shape = (rows, tokens)
    row_at = lax.broadcasted_iota(jnp.int32, shape, 0) + me * rows
    col_at = lax.broadcasted_iota(jnp.int32, shape, 1)
    seg_all = jnp.broadcast_to(seg, shape)
    own_seg = jnp.sum(jnp.where(row_at == col_at, seg_all, 0.0), axis=1, keepdims=True)
    count = jnp.sum(jnp.where(seg_all == own_seg, 1.0, 0.0), axis=1, keepdims=True)
    weights = tokens / (SEGS * count)
    attn_t[...] = flat(attn[...]).T
    total[...] = jnp.zeros_like(total)

    for step in range(1, chunks + len(stages) - 1):
        for j, stage in enumerate(stages):
            k = step - j
            if j == 0:
                k = step + ahead - 1
            if 0 <= k < chunks:
                stage(k)

    attn_grad[...] = (total[...] * scaling).astype(BF16)
    store("attn_grad", attn_grad, attn_grad_hbm, 3 * chunks)
    for copy in copies.values():
        copy.wait_send()
    for copy in stores:
        copy.wait()


def fused(attn, proj, mom, seg, target, radices, replicas, mixing):
    size, rows, wide = target.shape
    tokens, depth = size * rows, proj.shape[0]
    chunks = CHUNKS
    width = wide // chunks
    levels = len(radices)
    local = min(2, levels)
    most = max(radices) - 1
    scaling = (depth * size) ** (-0.5)
    dims = tuple(reversed(radices))
    sums, landed = [], []
    for level in range(local, levels):
        high = tuple(reversed(radices[level + 1 :]))
        sums.append(pltpu.VMEM((chunks,) + high + (radices[level], rows, width), BF16))
        landed.append(pltpu.VMEM((chunks, radices[level] - 1) + high + (rows, width), BF16))
    outer_dims, local_dims = dims[: levels - local], dims[levels - local :]
    group = 1
    for radix in local_dims:
        group *= radix
    any_place = pl.BlockSpec(memory_space=pl.ANY)
    dma = pltpu.SemaphoreType.DMA
    return pl.pallas_call(
        functools.partial(kernel, radices, local, replicas, chunks, mixing, scaling),
        out_shape=(
            jax.ShapeDtypeStruct((rows, wide), BF16),
            jax.ShapeDtypeStruct((tokens, depth), BF16),
            jax.ShapeDtypeStruct((depth, wide), BF16),
            jax.ShapeDtypeStruct((depth, wide), BF16),
        ),
        in_specs=[
            any_place,
            any_place,
            any_place,
            pl.BlockSpec(memory_space=pltpu.VMEM),
            any_place,
        ],
        out_specs=(any_place,) * 4,
        scratch_shapes=sums
        + landed
        + [
            pltpu.VMEM(dims + (rows, depth), BF16),
            pltpu.VMEM(local_dims + outer_dims + (rows, depth), BF16),
            pltpu.VMEM((chunks,) + local_dims + (depth, width), BF16),
            pltpu.VMEM((depth, wide), BF16),
            pltpu.VMEM((rows, wide), BF16),
            pltpu.VMEM((chunks,) + dims + (rows, width), BF16),
            pltpu.VMEM((chunks, depth, width), BF16),
            pltpu.VMEM((chunks, depth, width), BF16),
            pltpu.VMEM((depth, wide), BF16),
            pltpu.VMEM((depth, tokens), BF16),
            pltpu.VMEM((tokens, depth), F32),
            pltpu.VMEM((chunks, rows, width), BF16),
            pltpu.VMEM((tokens, depth), BF16),
            pltpu.VMEM((chunks, depth, width), BF16),
            pltpu.VMEM((chunks, depth, width), BF16),
            dma((3,)),
            dma((chunks,)),
            dma((3 * chunks + 1,)),
            dma((group,)),
            dma((group,)),
            dma((levels, chunks, most)),
            dma((levels, chunks, most)),
            dma((levels, chunks, most)),
            dma((levels, chunks, most)),
            dma((levels, chunks, most)),
            dma((levels, chunks, most)),
            dma((chunks + 1,)),
            dma((chunks + 1,)),
        ],
        cost_estimate=pl.CostEstimate(
            flops=6 * tokens * depth * wide, bytes_accessed=8 * depth * wide, transcendentals=0
        ),
        compiler_params=pltpu.CompilerParams(
            collective_id=0, has_side_effects=True, vmem_limit_bytes=VMEM_BYTES
        ),
    )(attn.reshape(dims + (rows, depth)), proj, mom, seg, target)


def passed_along(x, axis, by):
    size = lax.axis_size(axis)
    return lax.ppermute(x, axis, [(i, (i + by) % size) for i in range(size)])


def on_device(attn_out, proj, momentum, target, segment_ids, step):
    tensor_size = lax.axis_size("tensor")
    replicas = lax.axis_size("replica")
    rows_each = target.shape[1] // tensor_size
    bits = replicas.bit_length() - 1
    projected, attn_grad, updated, moment = fused(
        attn_out[0],
        proj[0],
        momentum[0],
        segment_ids,
        target[0].reshape(tensor_size, rows_each, target.shape[2]),
        radices_of(tensor_size),
        replicas,
        replicas == 2,
    )
    if replicas > 2:
        stacked = jnp.stack((updated, moment))
        branches = [
            partial(passed_along, axis="replica", by=1 << bit_pos) for bit_pos in range(bits)
        ]
        partner = lax.switch(step[0] % bits, branches, stacked)
        mixed = ((stacked.astype(F32) + partner.astype(F32)) * 0.5).astype(BF16)
        updated, moment = mixed[0], mixed[1]
    return (projected[None], attn_grad[None], updated[None], moment[None])


def solution(mesh):
    return jax.shard_map(
        on_device,
        mesh=mesh,
        in_specs=(
            P("replica", None, "tensor"),
            P("replica", "tensor", None),
            P("replica", "tensor", None),
            P("replica", None, None),
            P("replica", None),
            P(),
        ),
        out_specs=(
            P("replica", "tensor", None),
            P("replica", None, "tensor"),
            P("replica", "tensor", None),
            P("replica", "tensor", None),
        ),
        check_vma=False,
    )
```

time: 187 us -> 68 us (0.36)
  waiting for transfers between devices: 154 us -> 0 us
  Pallas kernels: 0 us -> 60.1 us
  between operations: 14.1 us -> 0.64 us
  matrix products: 9.25 us -> 0 us
  other arithmetic: 2.94 us -> 0 us
  local copies, waits for them, and re-layouts: 4.25 us -> 6.99 us
    reduce_scatter x1 -> x0, waiting for transfers between devices: 86.9 us -> none  [on_device(): lax.psum_scatter(jnp.dot(heads_in, weight, preferred_element_type=jnp.flo...]
    pallas_call x0 -> x1, Pallas kernels: none -> 60.1 us  [fused(): pl.pallas_call(functools.partial(kernel, radices, local, replicas, chunks...]
    all_gather x1 -> x0, waiting for transfers between devices: 44.9 us -> none  [on_device(): grad_block = lax.all_gather(grad_shard, 'tensor', axis=0, tiled=True)]
    ppermute x1 -> x0, waiting for transfers between devices: 22.1 us -> none  [passed_along(): return lax.ppermute(x, axis, [(i, (i + by) % size) for i in range(size)])]
    dot_general x3 -> x0, matrix products: 9.25 us -> none  [the longest x1 4.66 us: on_device(): jnp.dot(heads_in, weight, preferred_element_type=jnp.float32) * scaling]
    unnamed x14 -> x4, local copies, waits for them, and re-layouts: 4.1 us -> 6.99 us
    convert_element_type x2 -> x0, other arithmetic: 2.27 us -> none  [the longest x1 1.93 us: on_device(): ((own_sums - own_targets.astype(jnp.float32)) * own_weights[:, None]).ast...]
  transfers between devices with their start and end apart: 3 -> 0, of which waited for: 3 -> 0; matrix products, arithmetic and copies ran while one was open for 1% -> 0% of each run, Pallas kernels for 0% -> 0%
where the time goes in v2:
time: 68 us; the launch traced here: 67.7 us
  Pallas kernels  60.1 us (88%)
  local copies, waits for them, and re-layouts  6.99 us (10%)
    pallas_call x1, Pallas kernels, fused(): pl.pallas_call(functools.partial(kernel, radices, local, replicas, chunks...  60.1 us
    unnamed x4, local copies, waits for them, and re-layouts  6.99 us

profile of v2, /device:TPU:0, one launch (start us, length us, event | category | flops | bytes accessed | tf_op | source)
XLA Modules:
  0.0 67.7 jit_solution(5687615728324562222)
XLA Ops:
  0.6 60.1 %shard_map.84 = (bf16[48,2048]{1,0:T(8,128)(2,1)}, bf16[768,128]{1,0:T(8,128)(2,1)}, bf16[128,2048]{1,0:T(8,128)(2,1)}, bf16[128,2048]{1,0:T(8,128)(2,1)}) custom-call(bf16[2,2,2,2,48,128]{5,4,3,2,1,0:T(8,128)(2,1)} %bitcast.15, bf16[128,2048]{1,0:T(8,128)(2,1)} %bitcast.13, bf16[128,2048]{1,0:T(8,128)(2,1)} %bitcast.14, s32[1,768]{1,0:T(1,128)} %seg_ref.1, ...), custom_call_target="tpu_custom_call" | custom-call | flops 1207959552 | bytes 2097152 | tf_op jit(solution)/shard_map/pallas_call | solution.py:389
  60.7 1.6 %copy.13 = bf16[1,48,2048]{2,1,0:T(8,128)(2,1)} copy(bf16[1,48,2048]{2,1,0:T(8,128)(2,1)} %bitcast.11) | data formatting | bytes 393216
  62.3 1.6 %copy.14 = bf16[1,768,128]{2,1,0:T(8,128)(2,1)} copy(bf16[1,768,128]{2,1,0:T(8,128)(2,1)} %bitcast.10) | data formatting | bytes 393216
  63.9 1.9 %copy.15 = bf16[1,128,2048]{2,1,0:T(8,128)(2,1)} copy(bf16[1,128,2048]{2,1,0:T(8,128)(2,1)} %bitcast.9) | data formatting | bytes 1048576
  65.8 1.9 %copy.16 = bf16[1,128,2048]{2,1,0:T(8,128)(2,1)} copy(bf16[1,128,2048]{2,1,0:T(8,128)(2,1)} %bitcast.8) | data formatting | bytes 1048576

commit v3 on v2

--- a/solution.py
+++ b/solution.py
@@ -13,8 +13,9 @@
 BETA_MOM = 0.9
 STEP_RATE = 0.1
 CHUNKS = 8
-AHEAD = 4
-VMEM_BYTES = 63 * 1024 * 1024
+HOP_US = 1.5
+LINK_GB = 100.0
+VMEM_BYTES = 52 * 1024 * 1024
 BF16 = jnp.bfloat16
 F32 = jnp.float32
 MESH = pl.DeviceIdType.MESH
@@ -28,6 +29,56 @@
     if size > 1:
         found.append(size)
     return tuple(found)
+
+
+def hops_of(radices, local, replicas, chunks, rows, depth, width):
+    levels = len(radices)
+    block = 2e-6 * rows * width / LINK_GB
+    weight = 2e-6 * depth * width / LINK_GB
+    hops = []
+
+    def add(level, time, work):
+        chip = level > 0
+        hops.append((level, 1e3 * time * (2 if chip else 1 / 6), work))
+
+    for level in range(local - 1, -1, -1):
+        held = 1
+        for radix in radices[level + 1 : local]:
+            held *= radix
+        add(level, weight * held, 0.2)
+    size = 1
+    for radix in radices[local:]:
+        size *= radix
+    for level in range(local, levels):
+        size //= radices[level]
+        far = min(2, level - local + 1)
+        add(level if level == local else local, block * size * far, 0.3)
+    held = 1
+    for level in range(levels - 1, -1, -1):
+        far = 2 if level > local else 1
+        add(min(level, local), block * held * far, 0.3)
+        held *= radices[level]
+    hops.append(("y", 2e3 * weight, 0.6))
+    return hops
+
+
+def order_of(hops, chunks):
+    free, now, order = {}, 0.0, []
+    ready = {(0, k): 0.0 for k in range(chunks)}
+    while ready:
+        task = min(ready, key=lambda at: (max(ready[at], now), -at[0] if at[0] else 1, at[1]))
+        stage, k = task
+        now = max(now, ready.pop(task))
+        order.append(task)
+        if stage < len(hops):
+            link, time, work = hops[stage]
+            now += work
+            begin = max(now, free.get(link, 0.0))
+            free[link] = begin + time
+            ready[stage + 1, k] = begin + time + HOP_US
+        else:
+            now += 0.3
+    return order
 
 
 def kernel(
@@ -324,9 +375,11 @@
     stages += [partial(gather_stage, level) for level in range(levels - 1, -1, -1)]
     stages += [mix_stage]
 
-    ahead = min(AHEAD, chunks)
-    for k in range(ahead):
-        first(k)
+    order = order_of(hops_of(radices, local, replicas, chunks, rows, depth, width), chunks)
+    ahead = 0
+    while ahead < len(order) and order[ahead][0] == 0:
+        first(order[ahead][1])
+        ahead += 1
     if mixing:
         send(
             "yp",
@@ -349,13 +402,8 @@
     attn_t[...] = flat(attn[...]).T
     total[...] = jnp.zeros_like(total)
 
-    for step in range(1, chunks + len(stages) - 1):
-        for j, stage in enumerate(stages):
-            k = step - j
-            if j == 0:
-                k = step + ahead - 1
-            if 0 <= k < chunks:
-                stage(k)
+    for j, k in order[ahead:]:
+        stages[j](k)
 
     attn_grad[...] = (total[...] * scaling).astype(BF16)
     store("attn_grad", attn_grad, attn_grad_hbm, 3 * chunks)

time: 68 us -> 66.5 us (0.978)
  local copies, waits for them, and re-layouts: 6.99 us -> 4.54 us
  Pallas kernels: 60.1 us -> 61.1 us
    unnamed x4 -> x8, local copies, waits for them, and re-layouts: 6.99 us -> 4.54 us
    pallas_call x1, Pallas kernels: 60.1 us -> 61.1 us  [fused(): pl.pallas_call(functools.partial(kernel, radices, local, replicas, chunks...]
where the time goes in v3:
time: 66.5 us; the launch traced here: 66.3 us
  Pallas kernels  61.1 us (92%)
  local copies, waits for them, and re-layouts  4.54 us (7%)
    pallas_call x1, Pallas kernels, fused(): pl.pallas_call(functools.partial(kernel, radices, local, replicas, chunks...  61.1 us
    unnamed x8, local copies, waits for them, and re-layouts  4.54 us

profile of v3, /device:TPU:0, one launch (start us, length us, event | category | flops | bytes accessed | tf_op | source)
XLA Modules:
  0.0 66.3 jit_solution(12697588145582903399)
XLA Ops:
  0.6 0.0 copy-start
  0.6 0.9 %copy-done = bf16[1,768,128]{2,1,0:T(8,128)(2,1)S(1)} copy-done((bf16[1,768,128]{2,1,0:T(8,128)(2,1)S(1)}, bf16[1,768,128]{2,1,0:T(8,128)(2,1)}, u32[]{:S(2)}) %copy-start) | copy-done | bytes 196632
  1.6 0.0 copy-start.1
  1.6 0.7 %copy-done.1 = s32[1,768]{1,0:T(1,128)S(1)} copy-done((s32[1,768]{1,0:T(1,128)S(1)}, s32[1,768]{1,0:T(1,128)}, u32[]{:S(2)}) %copy-start.1) | copy-done | bytes 3096
  2.2 61.1 %shard_map.84 = (bf16[48,2048]{1,0:T(8,128)(2,1)S(1)}, bf16[768,128]{1,0:T(8,128)(2,1)S(1)}, bf16[128,2048]{1,0:T(8,128)(2,1)S(1)}, bf16[128,2048]{1,0:T(8,128)(2,1)S(1)}) custom-call(bf16[2,2,2,2,48,128]{5,4,3,2,1,0:T(8,128)(2,1)S(1)} %bitcast.12, bf16[128,2048]{1,0:T(8,128)(2,1)} %bitcast.14, bf16[128,2048]{1,0:T(8,128)(2,1)} %bitcast.15, ...), custom_call_target="tpu_custom_call" | custom-call | flops 1207959552 | bytes 2097152 | tf_op jit(solution)/shard_map/pallas_call | solution.py:437
  63.4 0.7 %copy.13 = bf16[1,48,2048]{2,1,0:T(8,128)(2,1)} copy(bf16[1,48,2048]{2,1,0:T(8,128)(2,1)S(1)} %bitcast.11) | data formatting | bytes 393216
  64.0 0.7 %copy.14 = bf16[1,768,128]{2,1,0:T(8,128)(2,1)} copy(bf16[1,768,128]{2,1,0:T(8,128)(2,1)S(1)} %bitcast.10) | data formatting | bytes 393216
  64.7 0.8 %copy.15 = bf16[1,128,2048]{2,1,0:T(8,128)(2,1)} copy(bf16[1,128,2048]{2,1,0:T(8,128)(2,1)S(1)} %bitcast.9) | data formatting | bytes 1048576
  65.5 0.8 %copy.16 = bf16[1,128,2048]{2,1,0:T(8,128)(2,1)} copy(bf16[1,128,2048]{2,1,0:T(8,128)(2,1)S(1)} %bitcast.8) | data formatting | bytes 1048576
Async XLA Ops:
  0.6 0.9 %copy-start = (bf16[1,768,128]{2,1,0:T(8,128)(2,1)S(1)}, bf16[1,768,128]{2,1,0:T(8,128)(2,1)}, u32[]{:S(2)}) copy-start(bf16[1,768,128]{2,1,0:T(8,128)(2,1)} %param.6) | copy-start | bytes 589828
  1.6 0.7 %copy-start.1 = (s32[1,768]{1,0:T(1,128)S(1)}, s32[1,768]{1,0:T(1,128)}, u32[]{:S(2)}) copy-start(s32[1,768]{1,0:T(1,128)} %seg_ref.1) | copy-start | bytes 9220

commit v4 on v3

--- a/solution.py
+++ b/solution.py
@@ -33,32 +33,27 @@
 
 def hops_of(radices, local, replicas, chunks, rows, depth, width):
     levels = len(radices)
-    block = 2e-6 * rows * width / LINK_GB
-    weight = 2e-6 * depth * width / LINK_GB
-    hops = []
-
-    def add(level, time, work):
-        chip = level > 0
-        hops.append((level, 1e3 * time * (2 if chip else 1 / 6), work))
-
+    block = 2e-3 * rows * width / LINK_GB
+    weight = 2e-3 * depth * width / LINK_GB
+    outer = 1
+    for radix in radices[local:]:
+        outer *= radix
+    hops, held = [], 1
     for level in range(local - 1, -1, -1):
-        held = 1
-        for radix in radices[level + 1 : local]:
-            held *= radix
-        add(level, weight * held, 0.2)
-    size = 1
-    for radix in radices[local:]:
-        size *= radix
-    for level in range(local, levels):
-        size //= radices[level]
-        far = min(2, level - local + 1)
-        add(level if level == local else local, block * size * far, 0.3)
+        time = weight * held
+        hops.append((level, time * 2 if level else time / 6, 0.2))
+        held *= radices[level]
+    hops.append(("far", 2 * block * max(1, outer - 1) * 4 / 3, 0.6))
     held = 1
     for level in range(levels - 1, -1, -1):
-        far = 2 if level > local else 1
-        add(min(level, local), block * held * far, 0.3)
+        time = block * held
+        if level >= local:
+            last = level == levels - 1
+            hops.append(("far" if last else local, time * (4 if last else 2), 0.4 if last else 0.2))
+        else:
+            hops.append((level, time * 2 if level else time / 6, 0.2))
         held *= radices[level]
-    hops.append(("y", 2e3 * weight, 0.6))
+    hops.append(("y", 2 * weight, 0.8))
     return hops
 
 
@@ -93,17 +88,17 @@
     mom_hbm,
     seg_ref,
     target_hbm,
-    projected_hbm,
-    attn_grad_hbm,
-    out_proj_hbm,
-    out_mom_hbm,
+    projected_ref,
+    attn_grad_ref,
+    out_proj_ref,
+    out_mom_ref,
     *scratch,
 ):
     levels = len(radices)
     outer = levels - local
-    sums = scratch[:outer]
-    landed = scratch[outer : 2 * outer]
     (
+        sums,
+        landed,
         attn,
         attn_group,
         proj,
@@ -115,13 +110,8 @@
         partner_proj,
         attn_t,
         total,
-        projected,
-        attn_grad,
-        out_proj,
-        out_mom,
         in_sem,
         proj_sem,
-        out_sem,
         a_send,
         a_recv,
         p_send,
@@ -132,7 +122,7 @@
         ag_recv,
         y_send,
         y_recv,
-    ) = scratch[2 * outer :]
+    ) = scratch
     rows, depth = attn.shape[-2:]
     width = proj.shape[-1]
     me = lax.axis_index("tensor")
@@ -152,15 +142,20 @@
         to = lax.rem(digits[level] + by, radices[level])
         return to, me + (to - digits[level]) * strides[level]
 
-    group = []
-    for offsets in itertools.product(*[range(r) for r in reversed(radices[:local])]):
-        if any(offsets):
-            there, index = [], me
-            for level, by in zip(range(local - 1, -1, -1), offsets):
-                to, _ = peer(level, by)
-                there.append(to)
-                index = index + (to - digits[level]) * strides[level]
-            group.append((tuple(there), index))
+    def others(levels_of):
+        found = []
+        for offsets in itertools.product(*[range(radices[level]) for level in levels_of]):
+            if any(offsets):
+                there, index = [], me
+                for level, by in zip(levels_of, offsets):
+                    to, _ = peer(level, by)
+                    there.append(to)
+                    index = index + (to - digits[level]) * strides[level]
+                found.append((tuple(there), index))
+        return found
+
+    group = others(range(local - 1, -1, -1))
+    summers = others(range(levels - 1, local - 1, -1))
 
     other = {"replica": lax.rem(rep + 1, replicas)}
 
@@ -184,13 +179,11 @@
 
     barrier = pltpu.get_barrier_semaphore()
     greet = [{"tensor": index} for _, index in group]
-    for level in range(local, levels):
-        greet += [{"tensor": peer(level, by)[1]} for by in range(1, radices[level])]
+    greet += [{"tensor": index} for _, index in summers]
     if mixing:
         greet.append(other)
     for device in greet:
         pl.semaphore_signal(barrier, inc=1, device_id=device, device_id_type=MESH)
-    loads[0].wait()
     pl.semaphore_wait(barrier, len(greet))
 
     copies = {}
@@ -210,7 +203,7 @@
     for i, (there, index) in enumerate(group):
         send(
             ("a", i),
-            attn.at[outer_all + there],
+            attn_hbm.at[outer_all + there],
             attn_group.at[own],
             a_send.at[i],
             a_recv.at[i],
@@ -230,21 +223,31 @@
             )
 
     def share_proj(level, k):
+        if level == local - 1:
+            place = (k,) + own
+            for by in range(1, radices[level]):
+                send(
+                    ("p", level, k, by),
+                    proj_hbm.at[:, columns(k)],
+                    proj.at[place],
+                    p_send.at[level, k, by - 1],
+                    p_recv.at[level, k, by - 1],
+                    {"tensor": peer(level, by)[1]},
+                )
+            return
         gather("p", proj, (p_send, p_recv), level, k, (slice(None),) * (local - 1 - level))
 
     def share_grad(level, k):
         gather("g", grads, (ag_send, ag_recv), level, k, (slice(None),) * (levels - 1 - level))
 
-    def reduce_start(level, k):
-        high = (slice(None),) * (levels - 1 - level)
-        for by in range(1, radices[level]):
-            to, index = peer(level, by)
+    def reduce_start(k):
+        for i, (there, index) in enumerate(summers):
             send(
-                ("r", level, k, by),
-                sums[level - local].at[(k,) + high + (to,)],
-                landed[level - local].at[k, by - 1],
-                rs_send.at[level, k, by - 1],
-                rs_recv.at[level, k, by - 1],
+                ("r", i, k),
+                sums.at[(k,) + there],
+                landed.at[k, i],
+                rs_send.at[i, k],
+                rs_recv.at[i, k],
                 {"tensor": index},
             )
 
@@ -253,15 +256,17 @@
             copies[kind, level, k, by].wait_recv()
 
     def first(k):
-        proj_loads[k].wait()
         if local > 0:
             share_proj(local - 1, k)
 
     def proj_stage(level, k):
+        proj_loads[k].wait()
         wait_recv("p", level, k)
         share_proj(level - 1, k)
 
     def product(k):
+        if local < 2:
+            proj_loads[k].wait()
         if local > 0:
             wait_recv("p", 0, k)
         if k == 0:
@@ -273,11 +278,8 @@
             part = part + jnp.dot(flat(left), proj[(k,) + at], preferred_element_type=F32)
         shape = tuple(reversed(radices[local:])) + (rows, width)
         part = part.reshape(shape)
-        if outer > 0:
-            sums[0][k] = part.astype(BF16)
-            reduce_start(local, k)
-        else:
-            finish(part, k)
+        sums[k] = part.astype(BF16)
+        reduce_start(k)
 
     def flat(block):
         count = 1
@@ -287,17 +289,12 @@
             return block.astype(F32).reshape(count, block.shape[-1]).astype(BF16)
         return block.reshape(count, block.shape[-1])
 
-    def reduce_stage(level, k):
-        wait_recv("r", level, k)
-        high = (slice(None),) * (levels - 1 - level)
-        value = sums[level - local][(k,) + high + (digits[level],)].astype(F32)
-        for by in range(1, radices[level]):
-            value = value + landed[level - local][k, by - 1].astype(F32)
-        if level + 1 < levels:
-            sums[level + 1 - local][k] = value.astype(BF16)
-            reduce_start(level + 1, k)
-        else:
-            finish(value, k)
+    def reduce_stage(k):
+        value = sums[(k,) + mine[:outer]].astype(F32)
+        for i in range(len(summers)):
+            copies["r", i, k].wait_recv()
+            value = value + landed[k, i].astype(F32)
+        finish(value, k)
 
     def finish(value, k):
         if k == 0:
@@ -306,15 +303,7 @@
         grad = (summed - target[:, columns(k)].astype(F32)) * weights
         grads[(k,) + mine] = grad.astype(BF16)
         share_grad(levels - 1, k)
-        projected[k] = summed.astype(BF16)
-        store(("projected", k), projected.at[k], projected_hbm.at[:, columns(k)], 3 * k)
-
-    stores = []
-
-    def store(key, src, dst, place):
-        copy = pltpu.make_async_copy(src, dst, out_sem.at[place])
-        copy.start()
-        stores.append(copy)
+        projected_ref[:, columns(k)] = summed.astype(BF16)
 
     def gather_stage(level, k):
         wait_recv("g", level, k)
@@ -344,10 +333,8 @@
         )
 
     def put(k, new_proj, new_moment):
-        out_proj[k] = new_proj
-        out_mom[k] = new_moment
-        store(("proj", k), out_proj.at[k], out_proj_hbm.at[:, columns(k)], 3 * k + 1)
-        store(("mom", k), out_mom.at[k], out_mom_hbm.at[:, columns(k)], 3 * k + 2)
+        out_proj_ref[:, columns(k)] = new_proj
+        out_mom_ref[:, columns(k)] = new_moment
 
     def updated_of(weight, moment):
         return (weight.astype(F32) - STEP_RATE * moment.astype(F32)).astype(BF16)
@@ -371,7 +358,7 @@
     stages = [first]
     stages += [partial(proj_stage, level) for level in range(local - 1, 0, -1)]
     stages += [product]
-    stages += [partial(reduce_stage, level) for level in range(local, levels)]
+    stages += [reduce_stage]
     stages += [partial(gather_stage, level) for level in range(levels - 1, -1, -1)]
     stages += [mix_stage]
 
@@ -389,6 +376,7 @@
             y_recv.at[chunks],
             other,
         )
+    loads[0].wait()
     attn_group[own] = attn[outer_all + own]
 
     seg = seg_ref[...].astype(F32)
@@ -405,12 +393,9 @@
     for j, k in order[ahead:]:
         stages[j](k)
 
-    attn_grad[...] = (total[...] * scaling).astype(BF16)
-    store("attn_grad", attn_grad, attn_grad_hbm, 3 * chunks)
+    attn_grad_ref[...] = (total[...] * scaling).astype(BF16)
     for copy in copies.values():
         copy.wait_send()
-    for copy in stores:
-        copy.wait()
 
 
 def fused(attn, proj, mom, seg, target, radices, replicas, mixing):
@@ -423,15 +408,12 @@
     most = max(radices) - 1
     scaling = (depth * size) ** (-0.5)
     dims = tuple(reversed(radices))
-    sums, landed = [], []
-    for level in range(local, levels):
-        high = tuple(reversed(radices[level + 1 :]))
-        sums.append(pltpu.VMEM((chunks,) + high + (radices[level], rows, width), BF16))
-        landed.append(pltpu.VMEM((chunks, radices[level] - 1) + high + (rows, width), BF16))
     outer_dims, local_dims = dims[: levels - local], dims[levels - local :]
     group = 1
     for radix in local_dims:
         group *= radix
+    summers = size // group - 1
+    vmem = pl.BlockSpec(memory_space=pltpu.VMEM)
     any_place = pl.BlockSpec(memory_space=pl.ANY)
     dma = pltpu.SemaphoreType.DMA
     return pl.pallas_call(
@@ -446,13 +428,13 @@
             any_place,
             any_place,
             any_place,
-            pl.BlockSpec(memory_space=pltpu.VMEM),
+            vmem,
             any_place,
         ],
-        out_specs=(any_place,) * 4,
-        scratch_shapes=sums
-        + landed
-        + [
+        out_specs=(vmem,) * 4,
+        scratch_shapes=[
+            pltpu.VMEM((chunks,) + outer_dims + (rows, width), BF16),
+            pltpu.VMEM((chunks, max(1, summers), rows, width), BF16),
             pltpu.VMEM(dims + (rows, depth), BF16),
             pltpu.VMEM(local_dims + outer_dims + (rows, depth), BF16),
             pltpu.VMEM((chunks,) + local_dims + (depth, width), BF16),
@@ -464,19 +446,14 @@
             pltpu.VMEM((depth, wide), BF16),
             pltpu.VMEM((depth, tokens), BF16),
             pltpu.VMEM((tokens, depth), F32),
-            pltpu.VMEM((chunks, rows, width), BF16),
-            pltpu.VMEM((tokens, depth), BF16),
-            pltpu.VMEM((chunks, depth, width), BF16),
-            pltpu.VMEM((chunks, depth, width), BF16),
             dma((3,)),
             dma((chunks,)),
-            dma((3 * chunks + 1,)),
             dma((group,)),
             dma((group,)),
             dma((levels, chunks, most)),
             dma((levels, chunks, most)),
-            dma((levels, chunks, most)),
-            dma((levels, chunks, most)),
+            dma((max(1, summers), chunks)),
+            dma((max(1, summers), chunks)),
             dma((levels, chunks, most)),
             dma((levels, chunks, most)),
             dma((chunks + 1,)),

time: 66.5 us -> 70.4 us (1.059)
  Pallas kernels: 61.1 us -> 65.1 us
    pallas_call x1, Pallas kernels: 61.1 us -> 65.1 us  [fused(): pl.pallas_call(functools.partial(kernel, radices, local, replicas, chunks...]
where the time goes in v4:
time: 70.4 us; the launch traced here: 70.3 us
  Pallas kernels  65.1 us (92%)
  local copies, waits for them, and re-layouts  4.54 us (6%)
    pallas_call x1, Pallas kernels, fused(): pl.pallas_call(functools.partial(kernel, radices, local, replicas, chunks...  65.1 us
    unnamed x8, local copies, waits for them, and re-layouts  4.54 us

profile of v4, /device:TPU:0, one launch (start us, length us, event | category | flops | bytes accessed | tf_op | source)
XLA Modules:
  0.0 70.3 jit_solution(8441041456069565311)
XLA Ops:
  0.6 0.0 copy-start
  0.6 0.9 %copy-done = bf16[1,768,128]{2,1,0:T(8,128)(2,1)S(1)} copy-done((bf16[1,768,128]{2,1,0:T(8,128)(2,1)S(1)}, bf16[1,768,128]{2,1,0:T(8,128)(2,1)}, u32[]{:S(2)}) %copy-start) | copy-done | bytes 196632
  1.6 0.0 copy-start.1
  1.6 0.7 copy-done.1
  2.2 65.1 %shard_map.84 = (bf16[48,2048]{1,0:T(8,128)(2,1)S(1)}, bf16[768,128]{1,0:T(8,128)(2,1)S(1)}, bf16[128,2048]{1,0:T(8,128)(2,1)S(1)}, bf16[128,2048]{1,0:T(8,128)(2,1)S(1)}) custom-call(bf16[2,2,2,2,48,128]{5,4,3,2,1,0:T(8,128)(2,1)S(1)} %bitcast.12, bf16[128,2048]{1,0:T(8,128)(2,1)} %bitcast.14, bf16[128,2048]{1,0:T(8,128)(2,1)} %bitcast.15, ...), custom_call_target="tpu_custom_call" | custom-call | flops 1207959552 | bytes 2097152 | tf_op jit(solution)/shard_map/pallas_call | solution.py:419
  67.3 0.7 copy.13
  68.0 0.7 copy.14
  68.7 0.8 %copy.15 = bf16[1,128,2048]{2,1,0:T(8,128)(2,1)} copy(bf16[1,128,2048]{2,1,0:T(8,128)(2,1)S(1)} %bitcast.9) | data formatting | bytes 1048576
  69.5 0.8 %copy.16 = bf16[1,128,2048]{2,1,0:T(8,128)(2,1)} copy(bf16[1,128,2048]{2,1,0:T(8,128)(2,1)S(1)} %bitcast.8) | data formatting | bytes 1048576
Async XLA Ops:
  0.6 0.9 %copy-start = (bf16[1,768,128]{2,1,0:T(8,128)(2,1)S(1)}, bf16[1,768,128]{2,1,0:T(8,128)(2,1)}, u32[]{:S(2)}) copy-start(bf16[1,768,128]{2,1,0:T(8,128)(2,1)} %param.6) | copy-start | bytes 589828
  1.6 0.7 copy-start.1

commit v5 on v3

--- a/solution.py
+++ b/solution.py
@@ -14,6 +14,7 @@
 STEP_RATE = 0.1
 CHUNKS = 8
 HOP_US = 1.5
+AHEAD = 3
 LINK_GB = 100.0
 VMEM_BYTES = 52 * 1024 * 1024
 BF16 = jnp.bfloat16
@@ -64,12 +65,14 @@
 
 def order_of(hops, chunks):
     free, now, order = {}, 0.0, []
-    ready = {(0, k): 0.0 for k in range(chunks)}
+    ready = {(0, k): 0.0 for k in range(min(AHEAD, chunks))}
     while ready:
         task = min(ready, key=lambda at: (max(ready[at], now), -at[0] if at[0] else 1, at[1]))
         stage, k = task
         now = max(now, ready.pop(task))
         order.append(task)
+        if stage == 1 and k + AHEAD < chunks:
+            ready[0, k + AHEAD] = now
         if stage < len(hops):
             link, time, work = hops[stage]
             now += work
@@ -93,10 +96,10 @@
     mom_hbm,
     seg_ref,
     target_hbm,
-    projected_hbm,
-    attn_grad_hbm,
-    out_proj_hbm,
-    out_mom_hbm,
+    projected_ref,
+    attn_grad_ref,
+    out_proj_ref,
+    out_mom_ref,
     *scratch,
 ):
     levels = len(radices)
@@ -115,13 +118,8 @@
         partner_proj,
         attn_t,
         total,
-        projected,
-        attn_grad,
-        out_proj,
-        out_mom,
         in_sem,
         proj_sem,
-        out_sem,
         a_send,
         a_recv,
         p_send,
@@ -306,15 +304,16 @@
         grad = (summed - target[:, columns(k)].astype(F32)) * weights
         grads[(k,) + mine] = grad.astype(BF16)
         share_grad(levels - 1, k)
-        projected[k] = summed.astype(BF16)
-        store(("projected", k), projected.at[k], projected_hbm.at[:, columns(k)], 3 * k)
-
-    stores = []
-
-    def store(key, src, dst, place):
-        copy = pltpu.make_async_copy(src, dst, out_sem.at[place])
-        copy.start()
-        stores.append(copy)
+        if mixing:
+            send(
+                ("yp", k),
+                proj.at[(k,) + own],
+                partner_proj.at[k],
+                y_send.at[chunks + k],
+                y_recv.at[chunks + k],
+                other,
+            )
+        projected_ref[:, columns(k)] = summed.astype(BF16)
 
     def gather_stage(level, k):
         wait_recv("g", level, k)
@@ -344,10 +343,8 @@
         )
 
     def put(k, new_proj, new_moment):
-        out_proj[k] = new_proj
-        out_mom[k] = new_moment
-        store(("proj", k), out_proj.at[k], out_proj_hbm.at[:, columns(k)], 3 * k + 1)
-        store(("mom", k), out_mom.at[k], out_mom_hbm.at[:, columns(k)], 3 * k + 2)
+        out_proj_ref[:, columns(k)] = new_proj
+        out_mom_ref[:, columns(k)] = new_moment
 
     def updated_of(weight, moment):
         return (weight.astype(F32) - STEP_RATE * moment.astype(F32)).astype(BF16)
@@ -355,12 +352,11 @@
     def mix_stage(k):
         if not mixing:
             return
-        if k == 0:
-            copies["yp"].wait_recv()
+        copies["yp", k].wait_recv()
         copies["y", k].wait_recv()
         ours, theirs = moments[k], partner_moments[k]
         one = updated_of(proj[(k,) + own], ours).astype(F32)
-        two = updated_of(partner_proj[:, columns(k)], theirs).astype(F32)
+        two = updated_of(partner_proj[k], theirs).astype(F32)
         put(
             k,
             ((one + two) * 0.5).astype(BF16),
@@ -380,15 +376,6 @@
     while ahead < len(order) and order[ahead][0] == 0:
         first(order[ahead][1])
         ahead += 1
-    if mixing:
-        send(
-            "yp",
-            proj_hbm,
-            partner_proj,
-            y_send.at[chunks],
-            y_recv.at[chunks],
-            other,
-        )
     attn_group[own] = attn[outer_all + own]
 
     seg = seg_ref[...].astype(F32)
@@ -405,12 +392,9 @@
     for j, k in order[ahead:]:
         stages[j](k)
 
-    attn_grad[...] = (total[...] * scaling).astype(BF16)
-    store("attn_grad", attn_grad, attn_grad_hbm, 3 * chunks)
+    attn_grad_ref[...] = (total[...] * scaling).astype(BF16)
     for copy in copies.values():
         copy.wait_send()
-    for copy in stores:
-        copy.wait()
 
 
 def fused(attn, proj, mom, seg, target, radices, replicas, mixing):
@@ -432,6 +416,7 @@
     group = 1
     for radix in local_dims:
         group *= radix
+    vmem = pl.BlockSpec(memory_space=pltpu.VMEM)
     any_place = pl.BlockSpec(memory_space=pl.ANY)
     dma = pltpu.SemaphoreType.DMA
     return pl.pallas_call(
@@ -446,10 +431,10 @@
             any_place,
             any_place,
             any_place,
-            pl.BlockSpec(memory_space=pltpu.VMEM),
+            vmem,
             any_place,
         ],
-        out_specs=(any_place,) * 4,
+        out_specs=(vmem,) * 4,
         scratch_shapes=sums
         + landed
         + [
@@ -461,16 +446,11 @@
             pltpu.VMEM((chunks,) + dims + (rows, width), BF16),
             pltpu.VMEM((chunks, depth, width), BF16),
             pltpu.VMEM((chunks, depth, width), BF16),
-            pltpu.VMEM((depth, wide), BF16),
+            pltpu.VMEM((chunks, depth, width), BF16),
             pltpu.VMEM((depth, tokens), BF16),
             pltpu.VMEM((tokens, depth), F32),
-            pltpu.VMEM((chunks, rows, width), BF16),
-            pltpu.VMEM((tokens, depth), BF16),
-            pltpu.VMEM((chunks, depth, width), BF16),
-            pltpu.VMEM((chunks, depth, width), BF16),
             dma((3,)),
             dma((chunks,)),
-            dma((3 * chunks + 1,)),
             dma((group,)),
             dma((group,)),
             dma((levels, chunks, most)),
@@ -479,8 +459,8 @@
             dma((levels, chunks, most)),
             dma((levels, chunks, most)),
             dma((levels, chunks, most)),
-            dma((chunks + 1,)),
-            dma((chunks + 1,)),
+            dma((2 * chunks,)),
+            dma((2 * chunks,)),
         ],
         cost_estimate=pl.CostEstimate(
             flops=6 * tokens * depth * wide, bytes_accessed=8 * depth * wide, transcendentals=0

time: 66.5 us -> 66.2 us (level)
  no operation moved by 1% of the time
where the time goes in v5:
time: 66.2 us; the launch traced here: 66.1 us
  Pallas kernels  60.9 us (92%)
  local copies, waits for them, and re-layouts  4.54 us (7%)
    pallas_call x1, Pallas kernels, fused(): pl.pallas_call(functools.partial(kernel, radices, local, replicas, chunks...  60.9 us
    unnamed x8, local copies, waits for them, and re-layouts  4.54 us

profile of v5, /device:TPU:0, one launch (start us, length us, event | category | flops | bytes accessed | tf_op | source)
XLA Modules:
  0.0 66.1 jit_solution(6937706838210459429)
XLA Ops:
  0.6 0.0 copy-start
  0.6 0.9 %copy-done = bf16[1,768,128]{2,1,0:T(8,128)(2,1)S(1)} copy-done((bf16[1,768,128]{2,1,0:T(8,128)(2,1)S(1)}, bf16[1,768,128]{2,1,0:T(8,128)(2,1)}, u32[]{:S(2)}) %copy-start) | copy-done | bytes 196632
  1.6 0.0 copy-start.1
  1.6 0.7 %copy-done.1 = s32[1,768]{1,0:T(1,128)S(1)} copy-done((s32[1,768]{1,0:T(1,128)S(1)}, s32[1,768]{1,0:T(1,128)}, u32[]{:S(2)}) %copy-start.1) | copy-done | bytes 3096
  2.2 60.9 %shard_map.84 = (bf16[48,2048]{1,0:T(8,128)(2,1)S(1)}, bf16[768,128]{1,0:T(8,128)(2,1)S(1)}, bf16[128,2048]{1,0:T(8,128)(2,1)S(1)}, bf16[128,2048]{1,0:T(8,128)(2,1)S(1)}) custom-call(bf16[2,2,2,2,48,128]{5,4,3,2,1,0:T(8,128)(2,1)S(1)} %bitcast.12, bf16[128,2048]{1,0:T(8,128)(2,1)} %bitcast.14, bf16[128,2048]{1,0:T(8,128)(2,1)} %bitcast.15, ...), custom_call_target="tpu_custom_call" | custom-call | flops 1207959552 | bytes 2097152 | tf_op jit(solution)/shard_map/pallas_call | solution.py:422
  63.1 0.7 %copy.13 = bf16[1,48,2048]{2,1,0:T(8,128)(2,1)} copy(bf16[1,48,2048]{2,1,0:T(8,128)(2,1)S(1)} %bitcast.11) | data formatting | bytes 393216
  63.8 0.7 %copy.14 = bf16[1,768,128]{2,1,0:T(8,128)(2,1)} copy(bf16[1,768,128]{2,1,0:T(8,128)(2,1)S(1)} %bitcast.10) | data formatting | bytes 393216
  64.5 0.8 %copy.15 = bf16[1,128,2048]{2,1,0:T(8,128)(2,1)} copy(bf16[1,128,2048]{2,1,0:T(8,128)(2,1)S(1)} %bitcast.9) | data formatting | bytes 1048576
  65.3 0.8 %copy.16 = bf16[1,128,2048]{2,1,0:T(8,128)(2,1)} copy(bf16[1,128,2048]{2,1,0:T(8,128)(2,1)S(1)} %bitcast.8) | data formatting | bytes 1048576
Async XLA Ops:
  0.6 0.9 %copy-start = (bf16[1,768,128]{2,1,0:T(8,128)(2,1)S(1)}, bf16[1,768,128]{2,1,0:T(8,128)(2,1)}, u32[]{:S(2)}) copy-start(bf16[1,768,128]{2,1,0:T(8,128)(2,1)} %param.6) | copy-start | bytes 589828
  1.6 0.7 %copy-start.1 = (s32[1,768]{1,0:T(1,128)S(1)}, s32[1,768]{1,0:T(1,128)}, u32[]{:S(2)}) copy-start(s32[1,768]{1,0:T(1,128)} %seg_ref.1) | copy-start | bytes 9220

commit v6 on v5

--- a/solution.py
+++ b/solution.py
@@ -12,9 +12,9 @@
 SEGS = 96
 BETA_MOM = 0.9
 STEP_RATE = 0.1
-CHUNKS = 8
+CHUNKS = 16
 HOP_US = 1.5
-AHEAD = 3
+AHEAD = 5
 LINK_GB = 100.0
 VMEM_BYTES = 52 * 1024 * 1024
 BF16 = jnp.bfloat16

time: 66.2 us -> 81.5 us (1.23)
  Pallas kernels: 60.9 us -> 76.1 us
    pallas_call x1, Pallas kernels: 60.9 us -> 76.1 us  [fused(): pl.pallas_call(functools.partial(kernel, radices, local, replicas, chunks...]
where the time goes in v6:
time: 81.5 us; the launch traced here: 81.3 us
  Pallas kernels  76.1 us (93%)
  local copies, waits for them, and re-layouts  4.54 us (6%)
    pallas_call x1, Pallas kernels, fused(): pl.pallas_call(functools.partial(kernel, radices, local, replicas, chunks...  76.1 us
    unnamed x8, local copies, waits for them, and re-layouts  4.54 us

profile of v6, /device:TPU:0, one launch (start us, length us, event | category | flops | bytes accessed | tf_op | source)
XLA Modules:
  0.0 81.3 jit_solution(5149555079883704103)
XLA Ops:
  0.6 0.0 copy-start
  0.6 0.9 %copy-done = bf16[1,768,128]{2,1,0:T(8,128)(2,1)S(1)} copy-done((bf16[1,768,128]{2,1,0:T(8,128)(2,1)S(1)}, bf16[1,768,128]{2,1,0:T(8,128)(2,1)}, u32[]{:S(2)}) %copy-start) | copy-done | bytes 196632
  1.6 0.0 copy-start.1
  1.6 0.7 copy-done.1
  2.2 76.1 %shard_map.84 = (bf16[48,2048]{1,0:T(8,128)(2,1)S(1)}, bf16[768,128]{1,0:T(8,128)(2,1)S(1)}, bf16[128,2048]{1,0:T(8,128)(2,1)S(1)}, bf16[128,2048]{1,0:T(8,128)(2,1)S(1)}) custom-call(bf16[2,2,2,2,48,128]{5,4,3,2,1,0:T(8,128)(2,1)S(1)} %bitcast.12, bf16[128,2048]{1,0:T(8,128)(2,1)} %bitcast.14, bf16[128,2048]{1,0:T(8,128)(2,1)} %bitcast.15, ...), custom_call_target="tpu_custom_call" | custom-call | flops 1207959552 | bytes 2097152 | tf_op jit(solution)/shard_map/pallas_call | solution.py:422
  78.4 0.7 copy.13
  79.1 0.7 copy.14
  79.7 0.8 copy.15
  80.5 0.8 copy.16
Async XLA Ops:
  0.6 0.9 %copy-start = (bf16[1,768,128]{2,1,0:T(8,128)(2,1)S(1)}, bf16[1,768,128]{2,1,0:T(8,128)(2,1)}, u32[]{:S(2)}) copy-start(bf16[1,768,128]{2,1,0:T(8,128)(2,1)} %param.6) | copy-start | bytes 589828
  1.6 0.7 copy-start.1

commit v7 on v5

--- a/solution.py
+++ b/solution.py
@@ -12,7 +12,7 @@
 SEGS = 96
 BETA_MOM = 0.9
 STEP_RATE = 0.1
-CHUNKS = 8
+SHARES = (1, 1, 1, 1, 1, 1, 1, 1)
 HOP_US = 1.5
 AHEAD = 3
 LINK_GB = 100.0
@@ -32,7 +32,7 @@
     return tuple(found)
 
 
-def hops_of(radices, local, replicas, chunks, rows, depth, width):
+def hops_of(radices, local, rows, depth, width):
     levels = len(radices)
     block = 2e-6 * rows * width / LINK_GB
     weight = 2e-6 * depth * width / LINK_GB
@@ -63,8 +63,8 @@
     return hops
 
 
-def order_of(hops, chunks):
-    free, now, order = {}, 0.0, []
+def order_of(hops, shares):
+    free, now, order, chunks = {}, 0.0, [], len(shares)
     ready = {(0, k): 0.0 for k in range(min(AHEAD, chunks))}
     while ready:
         task = min(ready, key=lambda at: (max(ready[at], now), -at[0] if at[0] else 1, at[1]))
@@ -76,6 +76,7 @@
         if stage < len(hops):
             link, time, work = hops[stage]
             now += work
+            time = time * shares[k]
             begin = max(now, free.get(link, 0.0))
             free[link] = begin + time
             ready[stage + 1, k] = begin + time + HOP_US
@@ -88,7 +89,7 @@
     radices,
     local,
     replicas,
-    chunks,
+    widths,
     mixing,
     scaling,
     attn_hbm,
@@ -104,9 +105,10 @@
 ):
     levels = len(radices)
     outer = levels - local
-    sums = scratch[:outer]
-    landed = scratch[outer : 2 * outer]
     (
+        sums,
+        landed,
+        attn_raw,
         attn,
         attn_group,
         proj,
@@ -130,9 +132,9 @@
         ag_recv,
         y_send,
         y_recv,
-    ) = scratch[2 * outer :]
+    ) = scratch
     rows, depth = attn.shape[-2:]
-    width = proj.shape[-1]
+    chunks = len(widths)
     me = lax.axis_index("tensor")
     rep = lax.axis_index("replica")
     digits, strides, rest, stride = [], [], me, 1
@@ -142,19 +144,19 @@
         rest = lax.div(rest, radix)
         stride *= radix
     tokens = stride * rows
-    mine = tuple(reversed(digits))
-    own = tuple(reversed(digits[:local]))
-    outer_all = (slice(None),) * outer
+    mine = tuple(digits)
+    own = tuple(digits[:local])
+    blocks = list(itertools.product(*[range(radix) for radix in radices]))
 
     def peer(level, by):
         to = lax.rem(digits[level] + by, radices[level])
         return to, me + (to - digits[level]) * strides[level]
 
     group = []
-    for offsets in itertools.product(*[range(r) for r in reversed(radices[:local])]):
+    for offsets in itertools.product(*[range(r) for r in radices[:local]]):
         if any(offsets):
             there, index = [], me
-            for level, by in zip(range(local - 1, -1, -1), offsets):
+            for level, by in zip(range(local), offsets):
                 to, _ = peer(level, by)
                 there.append(to)
                 index = index + (to - digits[level]) * strides[level]
@@ -163,15 +165,15 @@
     other = {"replica": lax.rem(rep + 1, replicas)}
 
     def columns(k):
-        return slice(k * width, (k + 1) * width)
+        return slice(sum(widths[:k]), sum(widths[: k + 1]))
 
     loads = [
-        pltpu.make_async_copy(attn_hbm, attn, in_sem.at[0]),
+        pltpu.make_async_copy(attn_hbm, attn_raw, in_sem.at[0]),
         pltpu.make_async_copy(mom_hbm, mom, in_sem.at[1]),
         pltpu.make_async_copy(target_hbm.at[me], target, in_sem.at[2]),
     ]
     proj_loads = [
-        pltpu.make_async_copy(proj_hbm.at[:, columns(k)], proj.at[(k,) + own], proj_sem.at[k])
+        pltpu.make_async_copy(proj_hbm.at[:, columns(k)], proj[k].at[own], proj_sem.at[k])
         for k in range(chunks)
     ]
     loads[0].start()
@@ -189,6 +191,8 @@
     for device in greet:
         pl.semaphore_signal(barrier, inc=1, device_id=device, device_id_type=MESH)
     loads[0].wait()
+    for at in blocks:
+        attn[at] = attn_raw[tuple(reversed(at))]
     pl.semaphore_wait(barrier, len(greet))
 
     copies = {}
@@ -208,39 +212,38 @@
     for i, (there, index) in enumerate(group):
         send(
             ("a", i),
-            attn.at[outer_all + there],
+            attn.at[there],
             attn_group.at[own],
             a_send.at[i],
             a_recv.at[i],
             {"tensor": index},
         )
 
-    def gather(kind, ref, sems, level, k, high):
-        place = (k,) + high + tuple(digits[i] for i in range(level, -1, -1))
+    def gather(kind, ref, sems, level, k):
+        place = tuple(digits[: level + 1])
         for by in range(1, radices[level]):
             send(
                 (kind, level, k, by),
-                ref.at[place],
-                ref.at[place],
+                ref[k].at[place],
+                ref[k].at[place],
                 sems[0].at[level, k, by - 1],
                 sems[1].at[level, k, by - 1],
                 {"tensor": peer(level, by)[1]},
             )
 
     def share_proj(level, k):
-        gather("p", proj, (p_send, p_recv), level, k, (slice(None),) * (local - 1 - level))
+        gather("p", proj, (p_send, p_recv), level, k)
 
     def share_grad(level, k):
-        gather("g", grads, (ag_send, ag_recv), level, k, (slice(None),) * (levels - 1 - level))
+        gather("g", grads, (ag_send, ag_recv), level, k)
 
     def reduce_start(level, k):
-        high = (slice(None),) * (levels - 1 - level)
         for by in range(1, radices[level]):
             to, index = peer(level, by)
             send(
                 ("r", level, k, by),
-                sums[level - local].at[(k,) + high + (to,)],
-                landed[level - local].at[k, by - 1],
+                sums[level - local][k].at[to],
+                landed[level - local][k].at[by - 1],
                 rs_send.at[level, k, by - 1],
                 rs_recv.at[level, k, by - 1],
                 {"tensor": index},
@@ -265,14 +268,14 @@
         if k == 0:
             for i in range(len(group)):
                 copies["a", i].wait_recv()
-        part = jnp.zeros((tokens // len_group, width), F32)
-        for at in itertools.product(*[range(r) for r in reversed(radices[:local])]):
+        part = jnp.zeros((tokens // len_group, widths[k]), F32)
+        for at in itertools.product(*[range(r) for r in radices[:local]]):
             left = attn_group[at]
-            part = part + jnp.dot(flat(left), proj[(k,) + at], preferred_element_type=F32)
-        shape = tuple(reversed(radices[local:])) + (rows, width)
+            part = part + jnp.dot(flat(left), proj[k][at], preferred_element_type=F32)
+        shape = tuple(radices[local:]) + (rows, widths[k])
         part = part.reshape(shape)
         if outer > 0:
-            sums[0][k] = part.astype(BF16)
+            sums[0][k][...] = part.astype(BF16)
             reduce_start(local, k)
         else:
             finish(part, k)
@@ -287,12 +290,11 @@
 
     def reduce_stage(level, k):
         wait_recv("r", level, k)
-        high = (slice(None),) * (levels - 1 - level)
-        value = sums[level - local][(k,) + high + (digits[level],)].astype(F32)
+        value = sums[level - local][k][digits[level]].astype(F32)
         for by in range(1, radices[level]):
-            value = value + landed[level - local][k, by - 1].astype(F32)
+            value = value + landed[level - local][k][by - 1].astype(F32)
         if level + 1 < levels:
-            sums[level + 1 - local][k] = value.astype(BF16)
+            sums[level + 1 - local][k][...] = value.astype(BF16)
             reduce_start(level + 1, k)
         else:
             finish(value, k)
@@ -302,17 +304,8 @@
             loads[2].wait()
         summed = value * scaling
         grad = (summed - target[:, columns(k)].astype(F32)) * weights
-        grads[(k,) + mine] = grad.astype(BF16)
+        grads[k][mine] = grad.astype(BF16)
         share_grad(levels - 1, k)
-        if mixing:
-            send(
-                ("yp", k),
-                proj.at[(k,) + own],
-                partner_proj.at[k],
-                y_send.at[chunks + k],
-                y_recv.at[chunks + k],
-                other,
-            )
         projected_ref[:, columns(k)] = summed.astype(BF16)
 
     def gather_stage(level, k):
@@ -322,16 +315,16 @@
             return
         if k == 0:
             loads[1].wait()
-        block = flat(grads[k])
-        weight = proj[(k,) + own]
+        block = flat(grads[k][...])
+        weight = proj[k][own]
         gradient = jnp.dot(attn_t[...], block, preferred_element_type=F32) * scaling
         moment = (BETA_MOM * mom[:, columns(k)].astype(F32) + gradient).astype(BF16)
         if mixing:
-            moments[k] = moment
+            moments[k][...] = moment
             send(
                 ("y", k),
-                moments.at[k],
-                partner_moments.at[k],
+                moments[k],
+                partner_moments[k],
                 y_send.at[k],
                 y_recv.at[k],
                 other,
@@ -352,11 +345,12 @@
     def mix_stage(k):
         if not mixing:
             return
-        copies["yp", k].wait_recv()
+        if k == 0:
+            copies["yp"].wait_recv()
         copies["y", k].wait_recv()
-        ours, theirs = moments[k], partner_moments[k]
-        one = updated_of(proj[(k,) + own], ours).astype(F32)
-        two = updated_of(partner_proj[k], theirs).astype(F32)
+        ours, theirs = moments[k][...], partner_moments[k][...]
+        one = updated_of(proj[k][own], ours).astype(F32)
+        two = updated_of(partner_proj[:, columns(k)], theirs).astype(F32)
         put(
             k,
             ((one + two) * 0.5).astype(BF16),
@@ -371,12 +365,15 @@
     stages += [partial(gather_stage, level) for level in range(levels - 1, -1, -1)]
     stages += [mix_stage]
 
-    order = order_of(hops_of(radices, local, replicas, chunks, rows, depth, width), chunks)
+    shares = tuple(width / widths[0] for width in widths)
+    order = order_of(hops_of(radices, local, rows, depth, widths[0]), shares)
     ahead = 0
     while ahead < len(order) and order[ahead][0] == 0:
         first(order[ahead][1])
         ahead += 1
-    attn_group[own] = attn[outer_all + own]
+    if mixing:
+        send("yp", proj_hbm, partner_proj, y_send.at[chunks], y_recv.at[chunks], other)
+    attn_group[own] = attn[own]
 
     seg = seg_ref[...].astype(F32)
     shape = (rows, tokens)
@@ -392,27 +389,33 @@
     for j, k in order[ahead:]:
         stages[j](k)
 
-    attn_grad_ref[...] = (total[...] * scaling).astype(BF16)
+    for i, at in enumerate(blocks):
+        place = sum(digit * stride for digit, stride in zip(at, strides))
+        attn_grad_ref[place] = (total[i * rows : (i + 1) * rows, :] * scaling).astype(BF16)
     for copy in copies.values():
         copy.wait_send()
+
+
+def per_chunk(widths, shape):
+    return [pltpu.VMEM(tuple(shape) + (width,), BF16) for width in widths]
 
 
 def fused(attn, proj, mom, seg, target, radices, replicas, mixing):
     size, rows, wide = target.shape
     tokens, depth = size * rows, proj.shape[0]
-    chunks = CHUNKS
-    width = wide // chunks
+    widths = tuple(wide // sum(SHARES) * share for share in SHARES)
+    chunks = len(widths)
     levels = len(radices)
     local = min(2, levels)
     most = max(radices) - 1
     scaling = (depth * size) ** (-0.5)
-    dims = tuple(reversed(radices))
+    dims = tuple(radices)
     sums, landed = [], []
     for level in range(local, levels):
-        high = tuple(reversed(radices[level + 1 :]))
-        sums.append(pltpu.VMEM((chunks,) + high + (radices[level], rows, width), BF16))
-        landed.append(pltpu.VMEM((chunks, radices[level] - 1) + high + (rows, width), BF16))
-    outer_dims, local_dims = dims[: levels - local], dims[levels - local :]
+        high = dims[level + 1 :]
+        sums.append(per_chunk(widths, (radices[level],) + high + (rows,)))
+        landed.append(per_chunk(widths, (radices[level] - 1,) + high + (rows,)))
+    local_dims, outer_dims = dims[:local], dims[local:]
     group = 1
     for radix in local_dims:
         group *= radix
@@ -420,10 +423,10 @@
     any_place = pl.BlockSpec(memory_space=pl.ANY)
     dma = pltpu.SemaphoreType.DMA
     return pl.pallas_call(
-        functools.partial(kernel, radices, local, replicas, chunks, mixing, scaling),
+        functools.partial(kernel, radices, local, replicas, widths, mixing, scaling),
         out_shape=(
             jax.ShapeDtypeStruct((rows, wide), BF16),
-            jax.ShapeDtypeStruct((tokens, depth), BF16),
+            jax.ShapeDtypeStruct((size, rows, depth), BF16),
             jax.ShapeDtypeStruct((depth, wide), BF16),
             jax.ShapeDtypeStruct((depth, wide), BF16),
         ),
@@ -435,18 +438,19 @@
             any_place,
         ],
         out_specs=(vmem,) * 4,
-        scratch_shapes=sums
-        + landed
-        + [
+        scratch_shapes=[
+            sums,
+            landed,
+            pltpu.VMEM(tuple(reversed(dims)) + (rows, depth), BF16),
             pltpu.VMEM(dims + (rows, depth), BF16),
             pltpu.VMEM(local_dims + outer_dims + (rows, depth), BF16),
-            pltpu.VMEM((chunks,) + local_dims + (depth, width), BF16),
+            per_chunk(widths, local_dims + (depth,)),
             pltpu.VMEM((depth, wide), BF16),
             pltpu.VMEM((rows, wide), BF16),
-            pltpu.VMEM((chunks,) + dims + (rows, width), BF16),
-            pltpu.VMEM((chunks, depth, width), BF16),
-            pltpu.VMEM((chunks, depth, width), BF16),
-            pltpu.VMEM((chunks, depth, width), BF16),
+            per_chunk(widths, dims + (rows,)),
+            per_chunk(widths, (depth,)),
+            per_chunk(widths, (depth,)),
+            pltpu.VMEM((depth, wide), BF16),
             pltpu.VMEM((depth, tokens), BF16),
             pltpu.VMEM((tokens, depth), F32),
             dma((3,)),
@@ -459,8 +463,8 @@
             dma((levels, chunks, most)),
             dma((levels, chunks, most)),
             dma((levels, chunks, most)),
-            dma((2 * chunks,)),
-            dma((2 * chunks,)),
+            dma((chunks + 1,)),
+            dma((chunks + 1,)),
         ],
         cost_estimate=pl.CostEstimate(
             flops=6 * tokens * depth * wide, bytes_accessed=8 * depth * wide, transcendentals=0
@@ -468,7 +472,7 @@
         compiler_params=pltpu.CompilerParams(
             collective_id=0, has_side_effects=True, vmem_limit_bytes=VMEM_BYTES
         ),
-    )(attn.reshape(dims + (rows, depth)), proj, mom, seg, target)
+    )(attn.reshape(tuple(reversed(dims)) + (rows, depth)), proj, mom, seg, target)
 
 
 def passed_along(x, axis, by):
@@ -499,7 +503,8 @@
         partner = lax.switch(step[0] % bits, branches, stacked)
         mixed = ((stacked.astype(F32) + partner.astype(F32)) * 0.5).astype(BF16)
         updated, moment = mixed[0], mixed[1]
-    return (projected[None], attn_grad[None], updated[None], moment[None])
+    attn_grad = attn_grad.reshape(attn_out.shape)
+    return (projected[None], attn_grad, updated[None], moment[None])
 
 
 def solution(mesh):

time: 66.2 us -> 66.1 us (level)
  no operation moved by 1% of the time
where the time goes in v7:
time: 66.1 us; the launch traced here: 65.9 us
  Pallas kernels  60.7 us (92%)
  local copies, waits for them, and re-layouts  4.54 us (7%)
    pallas_call x1, Pallas kernels, fused(): pl.pallas_call(functools.partial(kernel, radices, local, replicas, widths...  60.7 us
    unnamed x8, local copies, waits for them, and re-layouts  4.54 us

profile of v7, /device:TPU:0, one launch (start us, length us, event | category | flops | bytes accessed | tf_op | source)
XLA Modules:
  0.0 65.9 jit_solution(5270450315795624296)
XLA Ops:
  0.6 0.0 copy-start
  0.6 0.9 %copy-done = bf16[1,768,128]{2,1,0:T(8,128)(2,1)S(1)} copy-done((bf16[1,768,128]{2,1,0:T(8,128)(2,1)S(1)}, bf16[1,768,128]{2,1,0:T(8,128)(2,1)}, u32[]{:S(2)}) %copy-start) | copy-done | bytes 196632
  1.6 0.0 copy-start.1
  1.6 0.7 %copy-done.1 = s32[1,768]{1,0:T(1,128)S(1)} copy-done((s32[1,768]{1,0:T(1,128)S(1)}, s32[1,768]{1,0:T(1,128)}, u32[]{:S(2)}) %copy-start.1) | copy-done | bytes 3096
  2.2 60.7 %shard_map.84 = (bf16[48,2048]{1,0:T(8,128)(2,1)S(1)}, bf16[16,48,128]{2,1,0:T(8,128)(2,1)S(1)}, bf16[128,2048]{1,0:T(8,128)(2,1)S(1)}, bf16[128,2048]{1,0:T(8,128)(2,1)S(1)}) custom-call(bf16[2,2,2,2,48,128]{5,4,3,2,1,0:T(8,128)(2,1)S(1)} %bitcast.12, bf16[128,2048]{1,0:T(8,128)(2,1)} %bitcast.14, bf16[128,2048]{1,0:T(8,128)(2,1)} %bitcast.15, ...), custom_call_target="tpu_custom_call" | custom-call | flops 1207959552 | bytes 2097152 | tf_op jit(solution)/shard_map/pallas_call | solution.py:425
  63.0 0.7 %copy.13 = bf16[1,48,2048]{2,1,0:T(8,128)(2,1)} copy(bf16[1,48,2048]{2,1,0:T(8,128)(2,1)S(1)} %bitcast.11) | data formatting | bytes 393216
  63.7 0.7 %copy.14 = bf16[1,768,128]{2,1,0:T(8,128)(2,1)} copy(bf16[1,768,128]{2,1,0:T(8,128)(2,1)S(1)} %bitcast.10) | data formatting | bytes 393216
  64.3 0.8 %copy.15 = bf16[1,128,2048]{2,1,0:T(8,128)(2,1)} copy(bf16[1,128,2048]{2,1,0:T(8,128)(2,1)S(1)} %bitcast.9) | data formatting | bytes 1048576
  65.1 0.8 %copy.16 = bf16[1,128,2048]{2,1,0:T(8,128)(2,1)} copy(bf16[1,128,2048]{2,1,0:T(8,128)(2,1)S(1)} %bitcast.8) | data formatting | bytes 1048576
Async XLA Ops:
  0.6 0.9 %copy-start = (bf16[1,768,128]{2,1,0:T(8,128)(2,1)S(1)}, bf16[1,768,128]{2,1,0:T(8,128)(2,1)}, u32[]{:S(2)}) copy-start(bf16[1,768,128]{2,1,0:T(8,128)(2,1)} %param.6) | copy-start | bytes 589828
  1.6 0.7 %copy-start.1 = (s32[1,768]{1,0:T(1,128)S(1)}, s32[1,768]{1,0:T(1,128)}, u32[]{:S(2)}) copy-start(s32[1,768]{1,0:T(1,128)} %seg_ref.1) | copy-start | bytes 9220

commit v8 on v7

--- a/solution.py
+++ b/solution.py
@@ -12,9 +12,9 @@
 SEGS = 96
 BETA_MOM = 0.9
 STEP_RATE = 0.1
-SHARES = (1, 1, 1, 1, 1, 1, 1, 1)
+SHARES = (1, 2, 2, 2, 1)
 HOP_US = 1.5
-AHEAD = 3
+AHEAD = 2
 LINK_GB = 100.0
 VMEM_BYTES = 52 * 1024 * 1024
 BF16 = jnp.bfloat16

time: 66.1 us -> 68.3 us (1.033)
  Pallas kernels: 60.7 us -> 62.9 us
    pallas_call x1, Pallas kernels: 60.7 us -> 62.9 us  [fused(): pl.pallas_call(functools.partial(kernel, radices, local, replicas, widths...]
where the time goes in v8:
time: 68.3 us; the launch traced here: 68.1 us
  Pallas kernels  62.9 us (92%)
  local copies, waits for them, and re-layouts  4.54 us (7%)
    pallas_call x1, Pallas kernels, fused(): pl.pallas_call(functools.partial(kernel, radices, local, replicas, widths...  62.9 us
    unnamed x8, local copies, waits for them, and re-layouts  4.54 us

profile of v8, /device:TPU:0, one launch (start us, length us, event | category | flops | bytes accessed | tf_op | source)
XLA Modules:
  0.0 68.1 jit_solution(10900342079337055102)
XLA Ops:
  0.6 0.0 copy-start
  0.6 0.9 %copy-done = bf16[1,768,128]{2,1,0:T(8,128)(2,1)S(1)} copy-done((bf16[1,768,128]{2,1,0:T(8,128)(2,1)S(1)}, bf16[1,768,128]{2,1,0:T(8,128)(2,1)}, u32[]{:S(2)}) %copy-start) | copy-done | bytes 196632
  1.6 0.0 copy-start.1
  1.6 0.7 %copy-done.1 = s32[1,768]{1,0:T(1,128)S(1)} copy-done((s32[1,768]{1,0:T(1,128)S(1)}, s32[1,768]{1,0:T(1,128)}, u32[]{:S(2)}) %copy-start.1) | copy-done | bytes 3096
  2.2 62.9 %shard_map.84 = (bf16[48,2048]{1,0:T(8,128)(2,1)S(1)}, bf16[16,48,128]{2,1,0:T(8,128)(2,1)S(1)}, bf16[128,2048]{1,0:T(8,128)(2,1)S(1)}, bf16[128,2048]{1,0:T(8,128)(2,1)S(1)}) custom-call(bf16[2,2,2,2,48,128]{5,4,3,2,1,0:T(8,128)(2,1)S(1)} %bitcast.12, bf16[128,2048]{1,0:T(8,128)(2,1)} %bitcast.14, bf16[128,2048]{1,0:T(8,128)(2,1)} %bitcast.15, ...), custom_call_target="tpu_custom_call" | custom-call | flops 1207959552 | bytes 2097152 | tf_op jit(solution)/shard_map/pallas_call | solution.py:425
  65.1 0.7 copy.13
  65.8 0.7 copy.14
  66.5 0.8 %copy.15 = bf16[1,128,2048]{2,1,0:T(8,128)(2,1)} copy(bf16[1,128,2048]{2,1,0:T(8,128)(2,1)S(1)} %bitcast.9) | data formatting | bytes 1048576
  67.3 0.8 %copy.16 = bf16[1,128,2048]{2,1,0:T(8,128)(2,1)} copy(bf16[1,128,2048]{2,1,0:T(8,128)(2,1)S(1)} %bitcast.8) | data formatting | bytes 1048576
Async XLA Ops:
  0.6 0.9 %copy-start = (bf16[1,768,128]{2,1,0:T(8,128)(2,1)S(1)}, bf16[1,768,128]{2,1,0:T(8,128)(2,1)}, u32[]{:S(2)}) copy-start(bf16[1,768,128]{2,1,0:T(8,128)(2,1)} %param.6) | copy-start | bytes 589828
  1.6 0.7 %copy-start.1 = (s32[1,768]{1,0:T(1,128)S(1)}, s32[1,768]{1,0:T(1,128)}, u32[]{:S(2)}) copy-start(s32[1,768]{1,0:T(1,128)} %seg_ref.1) | copy-start | bytes 9220
